TPU v7x, 32 devices: a whole 2x2x4 slice. The times are simulated.
32 devices in a mesh: section: 2 (over x), rep: 16 (over z, y, core).
Axes of the slice: x: 2, y: 2, z: 4, core: 2. Of those that a mesh axis runs over, the one named last changes fastest.
Arguments:
- ends_in: bfloat16 [2, 8192, 768], P('section', 'rep'), may hold values from -6 to 6
- lengths: int32 [16, 2, 4], P('rep'), may hold values from 0 to 256, as said below
- times: int32 [16, 2, 4], P('rep'), may hold values from 0 to 999
- norm_gain: bfloat16 [2, 768], P('section'), may hold values from 0.099609375 to 1.8984375
- attend_in: bfloat16 [2, 768, 2304], P('section'), may hold values from -0.21875 to 0.21875
- attend_out: bfloat16 [2, 768, 768], P('section'), may hold values from -1.25 to 1.25
- time_weight: bfloat16 [2, 128, 2304], P('section'), may hold values from -0.5 to 0.5
- time_bias: bfloat16 [2, 2304], P('section'), may hold values from -3 to 3
- expand_weight: bfloat16 [2, 768, 3072], P('section'), may hold values from -0.21875 to 0.21875
- expand_bias: bfloat16 [2, 3072], P('section'), may hold values from -3 to 3
- reduce_weight: bfloat16 [2, 3072, 768], P('section'), may hold values from -0.109375 to 0.109375
- reduce_bias: bfloat16 [2, 768], P('section'), may hold values from -3 to 3
Outputs:
- ends_out: bfloat16 [2, 8192, 768], P('section', 'rep')
- grad_norm_gain: float32 [2, 768], P('section', 'rep')
- grad_attend_in: float32 [2, 768, 2304], P('section', 'rep')
- grad_attend_out: float32 [2, 768, 768], P('section', 'rep')
- grad_time_weight: float32 [2, 128, 2304], P('section', 'rep')
- grad_time_bias: float32 [2, 2304], P('section', 'rep')
- grad_expand_weight: float32 [2, 768, 3072], P('section', 'rep')
- grad_expand_bias: float32 [2, 3072], P('section', 'rep')
- grad_reduce_weight: float32 [2, 3072, 768], P('section', 'rep')
- grad_reduce_bias: float32 [2, 768], P('section', 'rep')
Inputs may be any that keep to these rules, and one draw needn't show every extreme that they name: Each micro-batch's 4 lengths sum to 256: either one sequence of 256 tokens followed by zeros, or 4 sequences of 64 tokens; some micro-batch of some replica holds one sequence.
All inputs are finite; a program needn't handle non-finite values.
Results may differ from a plain program's by a relative error of at most 0.019.
Values may be sent and summed in bfloat16 or wider, within the bound.
No kernel may reach another device: no remote copies, remote signals or barrier semaphores. Data moves between devices by JAX's collectives and lax.ppermute only.
A program may use at most 192 MiB of HBM per device.

v0:
```python
from functools import partial
import inspect
import math

import jax
import jax.numpy as jnp
import numpy as np
from jax import lax
from jax.experimental import pallas as pl
from jax.experimental.pallas import tpu as pltpu
from jax.sharding import PartitionSpec as P

HEADS = 12
HEAD = 64
EMB = 128
SEGS = 4
ANY = pl.ANY
VMEM = pltpu.MemorySpace.VMEM
SMEM = pltpu.MemorySpace.SMEM
F32 = jnp.float32
BF16 = jnp.bfloat16
ROOT_HALF = 0.7071067811865476
ROOT_TAU = 0.3989422804014327
TILE = 384
TAIL_ROWS = 24
GAIN_ROWS = 16
EXTRA = 16


class Bag(dict):
    __getattr__ = dict.__getitem__


def dot(left, right, left_dim=1, right_dim=0):
    return lax.dot_general(
        left, right, (((left_dim,), (right_dim,)), ((), ())), preferred_element_type=F32
    )


def repeat(count, body):
    for i in range(count):
        body(i)


def steps_of(count, size, body):
    def several(i, _):
        for j in range(size):
            body(size * i + j)
        return _

    lax.fori_loop(0, count // size, several, 0)


def lanes(index, size, start=0):
    if isinstance(index, int):
        return slice(start + index * size, start + (index + 1) * size)
    return pl.ds(pl.multiple_of(start + index * size, size), size)


def swap_halves(values, low_half):
    forth = pltpu.roll(values, 128 - HEAD // 2, 1)
    back = pltpu.roll(values, HEAD // 2, 1)
    return jnp.where(low_half, forth, back)


def norm_parts(values):
    center = values - jnp.mean(values, axis=-1, keepdims=True)
    spread = jnp.mean(center * center, axis=-1, keepdims=True)
    factor = lax.rsqrt(spread + 1e-05)
    return center * factor, factor


def norm_back(grad, unit, factor):
    return factor * (
        grad
        - jnp.mean(grad, axis=-1, keepdims=True)
        - unit * jnp.mean(grad * unit, axis=-1, keepdims=True)
    )


class Held:
    def __init__(self, bufs, loads, stores, sems, pieces):
        self.bufs = bufs
        self.loads = loads
        self.stores = stores
        self.sems = sems
        self.pieces = pieces
        self.names = {id(buf): name for name, buf in bufs.items()}
        keys = [(name, j) for name in loads for j in range(self.parts_of(name))]
        self.spots = {key: n for n, key in enumerate(keys)}
        self.waiting = set(keys)
        self.pending = set(keys)
        self.leaving = {}

    def parts_of(self, name):
        return self.pieces[name][1] if name in self.pieces else 1

    def load(self, name, j):
        source, target = self.loads[name], self.bufs[name]
        if name in self.pieces:
            axis, count = self.pieces[name]
            size = target.shape[axis] // count
            at = (slice(None),) * axis + (pl.ds(j * size, size),)
            source, target = source.at[at], target.at[at]
        return pltpu.make_async_copy(source, target, self.sems.at[self.spots[(name, j)]])

    def store(self, name, n):
        at, target = self.stores[name][n]
        source = self.bufs[name] if at is None else self.bufs[name].at[at]
        return pltpu.make_async_copy(source, target, self.sems.at[self.leaving[(name, n)]])

    def keys(self, bufs, part):
        for buf in bufs:
            name = self.names[id(buf)]
            for j in range(self.parts_of(name)):
                if part in (None, j):
                    yield name, j

    def begin(self, *bufs, part=None):
        for key in self.keys(bufs, part):
            if key in self.waiting:
                self.waiting.remove(key)
                self.load(*key).start()

    def need(self, *bufs, part=None):
        self.begin(*bufs, part=part)
        for key in self.keys(bufs, part):
            if key in self.pending:
                self.pending.remove(key)
                self.load(*key).wait()

    def done(self, *bufs):
        for buf in bufs:
            name = self.names[id(buf)]
            for n in range(len(self.stores.get(name, ()))):
                self.leaving[(name, n)] = len(self.spots) + len(self.leaving)
                self.store(name, n).start()

    def finish(self):
        for name, n in self.leaving:
            self.store(name, n).wait()


class Layer:
    def __init__(self, sizes, slot, refs):
        self.span, self.width, self.hidden, self.count = sizes
        self.slot = slot
        (
            lengths, section, core, self.mods, self.tbias, self.trig, self.gain, self.ebias,
            self.rbias,
        ) = refs
        self.section = section[0]
        self.core = core[0]
        self.single = lengths[slot, 0] == self.span
        self.pairs = self.width // 128
        self.seg = self.span // SEGS
        self.step = self.width
        self.tiles = self.hidden // self.step
        place = lax.broadcasted_iota(jnp.int32, (self.span, 128), 1)
        self.low_half = place % HEAD < HEAD // 2
        self.low_head = place < HEAD
        row = lax.broadcasted_iota(jnp.int32, (1, 128), 1) // HEAD
        self.head_row = [(row == i).astype(F32).astype(BF16) for i in range(2)]
        self.blocks = [(b, slice(b * self.seg, (b + 1) * self.seg)) for b in range(SEGS)]

    def trig_pair(self):
        cos_all, sin_all = self.trig[0], self.trig[1]
        cos_cut = jnp.concatenate([cos_all[: self.seg]] * SEGS, axis=0)
        sin_cut = jnp.concatenate([sin_all[: self.seg]] * SEGS, axis=0)
        return jnp.where(self.single, cos_all, cos_cut), jnp.where(self.single, sin_all, sin_cut)

    def mod_row(self, block, part):
        row = self.slot * SEGS + jnp.where(self.single, 0, block)
        at = slice(part * self.width, (part + 1) * self.width)
        return self.mods[pl.ds(row, 1), at] + self.tbias[:, at].astype(F32)

    def add_segment(self, small, block, at, sums):
        row = 2 + jnp.where(self.single, 0, block)
        small[pl.ds(row, 1), at * self.width : (at + 1) * self.width] += sums

    def side(self, block):
        return self.core if block % 2 == 0 else 1 - self.core

    def put_left(self, left, base, values):
        turned = values.T
        if left.shape[0] == 1:
            left[0, 2 * base : 2 * base + self.width] = turned
            return
        lines = self.width // self.count
        for block in range(self.count):
            to = base + block // 2 * lines
            left[self.side(block), to : to + lines] = turned[block * lines : (block + 1) * lines]

    def put_active(self, left, j, values):
        turned = values.T
        if left.shape[0] == 1:
            left[0, lanes(j, self.step)] = turned
            return
        lines = self.hidden // self.count
        per = self.step // lines
        for n in range(per):
            to = lanes(j, lines * (per // 2), n // 2 * lines)
            to = slice(to.start, to.start + lines) if isinstance(j, int) else pl.ds(to.start, lines)
            left[self.side(n), to] = turned[n * lines : (n + 1) * lines]

    def thirds(self, index):
        return [lanes(index, 128, p * self.width) for p in range(3)]


def left_bases(width, hidden):
    return 0, hidden // 2, (hidden + width) // 2, (hidden + 2 * width) // 2


def forward(
    k, xv, win, wout, wex, wre, left, qkv, probs, middle, slope, branch, result, bias, normed,
    mixed, modded,
):
    span, width, held = k.span, k.width, k.held
    _, at_modded, at_mixed, at_normed = left_bases(width, k.hidden)
    held.begin(xv, win)
    held.need(xv)
    unit, _ = norm_parts(xv[...].astype(F32))
    normed[...] = (unit * k.gain[...].astype(F32)).astype(BF16)
    across = lax.broadcasted_iota(jnp.int32, (span, span), 0) // k.seg
    down = lax.broadcasted_iota(jnp.int32, (span, span), 1) // k.seg
    bias[...] = jnp.where((across == down) | k.single, 0.0, -1e30)
    held.need(win)
    held.begin(wout, wex, wre)
    cos_part, sin_part = k.trig_pair()
    for tile, factor in ((0, 0.125), (1, 1.0)):
        for i in range(width // 256):
            at = lanes(i, 256, tile * width)
            joint = dot(normed[...], win[:, at])
            outs = []
            for piece in (joint[:, :128], joint[:, 128:]):
                turned = piece * cos_part + swap_halves(piece, k.low_half) * sin_part
                outs.append((turned * factor).astype(BF16))
            qkv[:, at] = jnp.concatenate(outs, axis=1)
    qkv[:, 2 * width :] = dot(normed[...], win[:, 2 * width :]).astype(BF16)
    held.done(qkv)
    if k.kept:
        k.put_left(left, at_normed, normed[...])

    def heads(i):
        at = k.thirds(i)
        query, key, value = (qkv[:, a] for a in at)
        outs = []
        for h in range(2):
            scores = dot(key * k.head_row[h], query, 1, 1) + bias[...]
            top = jnp.max(scores, axis=0, keepdims=True)
            raised = jnp.exp(scores - top)
            total = jnp.sum(raised, axis=0, keepdims=True)
            prob = raised * (1.0 / total)
            if k.kept:
                probs[2 * i + h] = prob
            outs.append(dot(prob.astype(BF16), value, 0, 0))
        mixed[:, at[0]] = jnp.where(k.low_head, outs[0], outs[1]).astype(BF16)

    steps_of(k.pairs, k.heads_step, heads)
    held.done(probs)
    held.need(wout)
    middle[...] = xv[...].astype(F32) + dot(mixed[...], wout[...])
    held.done(middle)
    if k.kept:
        k.put_left(left, at_mixed, mixed[...])
    for b, rows in k.blocks:
        unit, _ = norm_parts(middle[rows])
        modded[rows] = (unit * (1.0 + k.mod_row(b, 0)) + k.mod_row(b, 1)).astype(BF16)
    if k.kept:
        k.put_left(left, at_modded, modded[...])
    held.need(wex, wre)
    branch[...] = jnp.broadcast_to(k.rbias[...].astype(F32), (span, width))

    def feed(j):
        at = lanes(j, k.step)
        pre = dot(modded[...], wex[:, at]) + k.ebias[:, at].astype(F32)
        area = 0.5 + 0.5 * lax.erf(pre * ROOT_HALF)
        out = (pre * area).astype(BF16)
        if k.kept:
            slope[:, at] = area + pre * (jnp.exp(pre * pre * -0.5) * ROOT_TAU)
            k.put_active(left, j, out)
        branch[...] += dot(out, wre[at, :])

    if k.heads_step == 1:
        steps_of(k.tiles, 1, feed)
    else:
        repeat(k.tiles, feed)
    held.done(slope, left, branch)
    for b, rows in k.blocks:
        result[rows] = (middle[rows] + k.mod_row(b, 2) * branch[rows]).astype(BF16)
    held.done(result)


def output(k, dyv, bg):
    k.held.need(dyv)
    for b, rows in k.blocks:
        bg[rows] = (dyv[rows].astype(F32) * k.mod_row(b, 2)).astype(BF16)
    k.held.done(bg)


def mlp(k, wre, wex, bg, slope, middle, branch, dyv, pa, middle_grad, small, acc):
    span, width, hidden, held = k.span, k.width, k.hidden, k.held
    small[...] = jnp.zeros(small.shape, F32)
    acc[...] = jnp.zeros(acc.shape, F32)
    held.begin(bg)
    for j in range(k.tiles):
        held.begin(wre, slope, wex, part=j)
    held.begin(middle, dyv, branch)
    held.need(bg)

    def feed(j):
        at = lanes(j, k.step)
        held.need(wre, slope, wex, part=j)
        grad = dot(bg[...], wre[at, :], 1, 1)
        pre_grad = (slope[:, at] * grad).astype(BF16)
        pa[:span, at] = pre_grad
        small[0:1, at] = jnp.sum(pre_grad.astype(F32), axis=0, keepdims=True)
        acc[...] += dot(pre_grad, wex[:, at], 1, 1)

    repeat(k.tiles, feed)
    held.need(middle, dyv, branch)
    total = jnp.zeros((1, width), F32)
    for b, rows in k.blocks:
        cotan = dyv[rows].astype(F32)
        total += jnp.sum(bg[rows].astype(F32), axis=0, keepdims=True)
        grad = acc[rows]
        unit, factor = norm_parts(middle[rows])
        k.add_segment(small, b, 0, jnp.sum(grad * unit, axis=0, keepdims=True))
        k.add_segment(small, b, 1, jnp.sum(grad, axis=0, keepdims=True))
        k.add_segment(small, b, 2, jnp.sum(cotan * branch[rows], axis=0, keepdims=True))
        back = norm_back(grad * (1.0 + k.mod_row(b, 0)), unit, factor)
        full = cotan + back
        middle_grad[rows] = full
        pa[rows, hidden:] = full.astype(BF16)
    small[1:2, :width] = total
    pa[span:, :] = small[...].astype(BF16)
    held.done(pa, middle_grad)


def attend(
    k, wout, win, agrad, probs, qkv, xv, middle_grad, jg, leave, mixed_grad, acc
):
    span, held = k.span, k.held
    held.need(agrad, wout)
    held.begin(probs, qkv)
    mixed_grad[...] = dot(agrad[...], wout[...], 1, 1).astype(BF16)
    held.need(probs, qkv)
    held.begin(win, xv, middle_grad)
    cos_part, sin_part = k.trig_pair()

    def heads(i):
        at = k.thirds(i)
        query, key, value = (qkv[:, a] for a in at)
        out_grad = mixed_grad[:, at[0]]
        parts = []
        for h in range(2):
            prob = probs[2 * i + h]
            pull = dot(value * k.head_row[h], out_grad, 1, 1)
            shared = jnp.sum(prob * pull, axis=0, keepdims=True)
            score_grad = (prob * (pull - shared)).astype(BF16)
            parts.append(
                (
                    dot(score_grad, key, 0, 0),
                    dot(score_grad, query),
                    dot(prob.astype(BF16), out_grad),
                )
            )
        for p in range(3):
            grad = jnp.where(k.low_head, parts[0][p], parts[1][p])
            if p < 2:
                grad = grad * cos_part - swap_halves(grad, k.low_half) * sin_part
                if p == 0:
                    grad = grad * 0.125
            jg[:span, at[p]] = grad.astype(BF16)

    steps_of(k.pairs, k.heads_step, heads)
    held.need(win, xv, middle_grad)
    acc[...] = dot(jg[:span, :], win[...], 1, 1)
    total = jnp.zeros((1, k.width), F32)
    for b, rows in k.blocks:
        grad = acc[rows]
        unit, factor = norm_parts(xv[rows].astype(F32))
        total += jnp.sum(grad * unit, axis=0, keepdims=True)
        back = norm_back(grad * k.gain[...].astype(F32), unit, factor)
        leave[rows] = (middle_grad[rows] + back).astype(BF16)
    below = jnp.concatenate([total, jnp.zeros((EXTRA - 1, k.width), F32)], axis=0)
    jg[span:, : k.width] = below.astype(BF16)
    jg[span:, k.width :] = jnp.zeros((EXTRA, 2 * k.width), BF16)
    held.done(jg, leave)


def copy_agrad(k, pa, agrad):
    agrad[...] = pa[: k.span, k.hidden :]


class Sums:
    def __init__(self, ranks, full, outs, sems):
        self.full = full
        self.own = [((ranks[0] >> bit) & 1) == 0 for bit in (1, 2)]
        self.bufs = outs[:4]
        self.targets = outs[4:]
        self.sems = sems
        self.half = full.shape[1] // 2
        self.copies = []

    def put(self, block, at, values):
        self.full[block, at] = values

    def settle(self, which, groups):
        send, keep = self.bufs[2 * which : 2 * which + 2]
        at = slice(which * self.half, (which + 1) * self.half)
        apart = 1 + which
        for group in groups:
            for n in range(2):
                first = 4 * group + (2 * n if which == 0 else n)
                even, odd = self.full[first, at], self.full[first + apart, at]
                send[2 * group + n] = jnp.where(self.own[which], odd, even).astype(BF16)
                keep[2 * group + n] = jnp.where(self.own[which], even, odd)
            spot = pl.ds(2 * group, 2)
            for n in range(2 * which, 2 * which + 2):
                copy = pltpu.make_async_copy(
                    self.bufs[n].at[spot], self.targets[n].at[spot], self.sems.at[len(self.copies)]
                )
                copy.start()
                self.copies.append(copy)

    def finish(self):
        for copy in self.copies:
            copy.wait()


def term_reduce(k, sums, left, right):
    lines = k.hidden // k.count
    per = TILE // lines
    for tile in range(k.hidden // 2 // TILE):
        k.arrive(tile)
        total = dot(left[tile * TILE : (tile + 1) * TILE], right[...])
        for n in range(per):
            sums.put(tile * per + n, slice(0, lines), total[n * lines : (n + 1) * lines])
        if (tile + 1) * per % 4 == 0:
            group = ((tile + 1) * per // 4 - 1,)
            sums.settle(0, group)
            sums.settle(1, group)


def square_terms(k, sums, left, right, cols, part):
    lines = k.width // k.count
    total = dot(left, right[: 4 * k.span, cols])
    for n in range(k.count // 2):
        sums.put(n, slice(part * lines, (part + 1) * lines), total[n * lines : (n + 1) * lines])


def term_expand(k, sums, left, right):
    width, hidden, span = k.width, k.hidden, k.span
    groups = range(k.count // 8)
    tall = hidden // width
    lines = width // k.count
    rows = width // 2
    half = sums.half
    settled = False
    for col in range(tall + 1):
        k.arrive(col)
        part = left[:rows] if col < tall else left[rows:]
        square_terms(k, sums, part, right, slice(col * width, (col + 1) * width), col)
        if (col + 1) * lines >= half and not settled:
            sums.settle(0, groups)
            settled = True
    smalls = [k.small[n].astype(F32) for n in range(4)]
    angles = jnp.concatenate([embed[...] for embed in k.embeds], axis=1)
    pieces = []
    for _ in range(3):
        pieces.append(angles.astype(BF16))
        angles = angles - pieces[-1].astype(F32)
    seqs = jnp.concatenate([small[2 : 2 + SEGS, : 3 * width] for small in smalls]).astype(BF16)
    times = sum(dot(piece, seqs) for piece in pieces)
    both = sum(smalls)
    seq_sum = jnp.sum(both[2 : 2 + SEGS, : 3 * width], axis=0, keepdims=True)
    lines_v = k.lines
    lines_v[...] = jnp.zeros(lines_v.shape, F32)
    lines_v[0:1] = both[1:2, :width]
    for n in range(3):
        lines_v[1 + n : 2 + n] = seq_sum[:, n * width : (n + 1) * width]
    for n in range(tall):
        lines_v[4 + n : 5 + n] = both[0:1, n * width : (n + 1) * width]
    deep = EMB // k.count
    first = (tall + 1) * lines
    low = k.core == 0
    for g in range(k.count // 2):
        for p in range(3):
            at = slice(p * width, (p + 1) * width)
            even = times[2 * g * deep : (2 * g + 1) * deep, at]
            odd = times[(2 * g + 1) * deep : (2 * g + 2) * deep, at]
            to = first + p * deep
            sums.put(g, slice(to, to + deep), jnp.where(low, even, odd))
        sums.put(g, slice(first + 3 * deep, 2 * half), lines_v[...])
    sums.settle(1, groups)


def term_attend(k, sums, left, right):
    width = k.width
    groups = range(k.count // 8)
    lines = width // k.count
    settled = False
    for col in range(3):
        k.arrive(col)
        square_terms(k, sums, left[...], right, slice(col * width, (col + 1) * width), col)
        if (col + 1) * lines >= sums.half and not settled:
            sums.settle(0, groups)
            settled = True
    gain = sum(k.small[n].astype(F32) for n in range(4))[:, :width]
    for g in range(k.count // 2):
        sums.put(g, slice(3 * lines, 3 * lines + GAIN_ROWS), gain)
    sums.settle(1, groups)


def load_terms(k, refs, bufs, base, sems):
    left_v, right_v, small_v = bufs
    rows, cols = left_v.shape[0], right_v.shape[1]
    tall = rows // TILE if small_v is None else 1
    wide = cols // k.width
    groups = []
    for i in range(tall):
        for j in range(wide):
            copies = []
            for n, (left, right) in enumerate(zip(refs[:4], refs[4:8])):
                tokens = pl.ds(n * k.span, k.span)
                part = pl.ds(i * (rows // tall), rows // tall)
                from_part = pl.ds(base + i * (rows // tall), rows // tall)
                at = pl.ds(j * k.width, k.width)
                if j == 0:
                    copies.append((left.at[from_part], left_v.at[part, tokens]))
                if i == 0:
                    copies.append((right.at[pl.ds(0, k.span), at], right_v.at[tokens, at]))
                if small_v is not None and j == wide - 1:
                    copies.append((right.at[pl.ds(k.span, EXTRA)], small_v.at[n]))
            groups.append(copies)
    made, count = [], 0
    for copies in groups:
        made.append([])
        for pair in copies:
            made[-1].append(pltpu.make_async_copy(*pair, sems.at[count]))
            made[-1][-1].start()
            count += 1
    return made


class Terms:
    def __init__(self, sizes, core):
        self.span, self.width, self.hidden, self.count = sizes
        self.core = core[0]

    def arrive(self, group):
        for copy in self.groups[group]:
            copy.wait()


def term_kernel(sizes, body, base, extra, *refs):
    refs = list(refs)
    core, rank = refs[:2]
    k = Terms(sizes, core)
    pos = 2
    if body is term_expand:
        k.embeds = refs[pos : pos + 2]
        pos += 2
    sources = refs[pos : pos + 8]
    pos += 8 + extra
    targets = refs[pos : pos + 4]
    pos += 4
    left_v, right_v, full, *outs = refs[pos : pos + 7]
    pos += 7
    k.small = None
    if body is not term_reduce:
        k.small, k.lines = refs[pos : pos + 2]
        pos += 2
    sems, out_sems = refs[pos:]
    k.groups = load_terms(k, sources, (left_v, right_v, k.small), base, sems)
    sums = Sums(rank, full, outs + targets, out_sems)
    body(k, sums, left_v, right_v)
    sums.finish()


def term_call(name, body, sizes, lines, base, rows, core, rank, lefts, rights, embeds=(), after=()):
    span, width, hidden, count = sizes
    blocks = count // 2
    cols = rights[0].shape[1]
    half = lines // 2
    outs = [((blocks // 2, half, width), kind) for kind in (BF16, F32)] * 2
    scratch = [
        ((rows, 4 * span), BF16),
        ((4 * span, cols), BF16),
        ((blocks, lines, width), F32),
        *outs,
    ]
    if body is not term_reduce:
        scratch += [((4, EXTRA, cols), BF16), ((TAIL_ROWS, width), F32)]
    args = [core.reshape(1), rank.reshape(1), *embeds, *lefts, *rights, *after]
    in_specs = [pl.BlockSpec(memory_space=SMEM)] * 2
    in_specs += [pl.BlockSpec(memory_space=VMEM)] * len(embeds)
    in_specs += [pl.BlockSpec(memory_space=ANY)] * (8 + len(after))
    return pl.pallas_call(
        partial(term_kernel, sizes, body, base, len(after)),
        out_shape=[jax.ShapeDtypeStruct(*item) for item in outs],
        in_specs=in_specs,
        out_specs=[pl.BlockSpec(memory_space=ANY)] * 4,
        scratch_shapes=[pltpu.VMEM(*item) for item in scratch]
        + [pltpu.SemaphoreType.DMA((32,)), pltpu.SemaphoreType.DMA((8,))],
        compiler_params=pltpu.CompilerParams(vmem_limit_bytes=62 * 1024 * 1024),
        name=name,
    )(*args)


def plain_pieces(lefts, rights, embed, sizes):
    span, width, hidden, count = sizes
    bg, pa, jg = rights
    bases = [2 * base for base in left_bases(width, hidden)]

    def blocks(base, rows, right):
        total = sum(dot(a[base : base + rows], b) for a, b in zip(lefts, right))
        parts = [total[:, i : i + width] for i in range(0, total.shape[1], width)]
        return [part.reshape(count, -1, width) for part in parts]

    take = lambda items, cols: [item[:span, cols] for item in items]
    reduce = blocks(bases[0], hidden, bg)
    expand = blocks(bases[1], width, take(pa, slice(0, hidden)))
    expand += blocks(bases[2], width, take(pa, slice(hidden, hidden + width)))
    last = blocks(bases[3], width, take(jg, slice(None)))
    small = [item[span:].astype(F32) for item in pa]
    seqs = jnp.concatenate([item[2 : 2 + SEGS, : 3 * width] for item in small])
    times = jnp.dot(embed, seqs, precision=lax.Precision.HIGHEST)
    expand += [times[:, i * width : (i + 1) * width].reshape(count, -1, width) for i in range(3)]
    lines = jnp.concatenate(
        [
            sum(item[1:2, :width] for item in small),
            jnp.sum(seqs, axis=0).reshape(-1, width),
            sum(item[0, :hidden] for item in small).reshape(-1, width),
        ]
    )
    lines = jnp.pad(lines, ((0, TAIL_ROWS - lines.shape[0]), (0, 0)))
    gain = sum(item[span:, :width].astype(F32) for item in jg)
    expand.append(jnp.broadcast_to(lines, (count,) + lines.shape))
    last.append(jnp.broadcast_to(gain, (count,) + gain.shape))
    return [jnp.concatenate(item, axis=1) for item in (reduce, expand, last)]


def shapes_of(span, width, hidden, cores):
    tok = lambda cols, kind=BF16: ((span, cols), kind)
    below = lambda cols: ((span + EXTRA, cols), BF16)
    return dict(
        xv=tok(width),
        dyv=tok(width),
        win=((width, 3 * width), BF16),
        wout=((width, width), BF16),
        wex=((width, hidden), BF16),
        wre=((hidden, width), BF16),
        left=((cores, (hidden + 3 * width) // cores, span), BF16),
        normed=tok(width),
        qkv=tok(3 * width),
        probs=((HEADS, span, span), F32),
        mixed=tok(width),
        middle=tok(width, F32),
        modded=tok(width),
        slope=tok(hidden, F32),
        branch=tok(width, F32),
        result=tok(width),
        bg=tok(width),
        pa=below(hidden + width),
        jg=below(3 * width),
        agrad=tok(width),
        mixed_grad=tok(width),
        middle_grad=tok(width, F32),
        leave=tok(width),
        acc=tok(width, F32),
        bias=tok(span, F32),
        small=((EXTRA, hidden + width), F32),
    )


def uses(part):
    return list(inspect.signature(part).parameters)[1:]


def stage_kernel(sizes, parts, who, slot, plan, *refs):
    refs = list(refs)
    layer = Layer(sizes, slot, refs[:9])
    span = layer.span
    pos = 9
    loads = {}
    for name, row, cols in plan.sources:
        ref = refs[pos]
        if cols is not None:
            ref = ref.at[pl.ds(0, span), pl.ds(*cols)]
        elif row is not None:
            ref = ref.at[pl.ds(row, span)]
        loads[name] = ref
        pos += 1
    pos += plan.extra
    stores = {}
    for name, row, at in plan.targets:
        target = refs[pos] if row is None else refs[pos].at[pl.ds(row, span)]
        stores.setdefault(name, []).append((at, target))
        pos += 1
    bufs = {}
    for name in plan.bufs:
        bufs[name] = refs[pos]
        pos += 1
    layer.held = Held(bufs, loads, stores, refs[pos], plan.pieces)
    layer.kept = plan.kept
    layer.heads_step = plan.heads_step

    @pl.when(layer.section == who)
    def _():
        for part in parts:
            part(layer, *[bufs[name] for name in uses(part)])
        layer.held.finish()


def stage(
    name, common, parts, who, slot, loads, stores, carried=None, after=(), kept=True, heads_step=3,
    pieces=None,
):
    carried = carried or {}
    span, width, hidden, count = common.sizes
    shapes = shapes_of(span, width, hidden, common.cores)
    bufs = []
    for part in parts:
        bufs += [item for item in uses(part) if item not in bufs]
    pair = lambda item: item if isinstance(item, tuple) else (item, None)
    args = list(common.args)
    in_specs = [pl.BlockSpec(memory_space=SMEM)] * 3 + [pl.BlockSpec(memory_space=VMEM)] * 6
    plan = Bag(sources=[], targets=[], bufs=bufs, kept=kept, heads_step=heads_step)
    plan["pieces"] = pieces or {}
    for item in loads:
        if item in bufs:
            array, row, *cols = pair(loads[item])
            args.append(array)
            plan.sources.append((item, row, cols[0] if cols else None))
    outs, aliases, extra = [], {}, []
    targets = []
    for item, key in stores.items():
        if item == "left":
            targets += [(item, key + "_send" * n, None, n) for n in range(common.cores)]
        else:
            targets.append((item, *pair(key), None))
    for i, (item, key, row, at) in enumerate(targets):
        shape, kind = shapes[item]
        if row is not None:
            shape = (common.tokens,) + shape[1:]
        if at is not None:
            shape = shape[1:]
        outs.append(jax.ShapeDtypeStruct(shape, kind))
        plan.targets.append((item, row, at))
        if key in carried:
            aliases[len(args) + len(extra)] = i
            extra.append(carried[key])
    extra += list(after)
    args += extra
    plan["extra"] = len(extra)
    in_specs += [pl.BlockSpec(memory_space=ANY)] * (len(args) - len(in_specs))
    results = pl.pallas_call(
        partial(stage_kernel, common.sizes, parts, who, slot, plan),
        out_shape=outs,
        in_specs=in_specs,
        out_specs=[pl.BlockSpec(memory_space=ANY)] * len(outs),
        input_output_aliases=aliases,
        scratch_shapes=[pltpu.VMEM(*shapes[item]) for item in bufs]
        + [pltpu.SemaphoreType.DMA((32,))],
        compiler_params=pltpu.CompilerParams(vmem_limit_bytes=62 * 1024 * 1024),
        name=name,
    )(*args)
    return Bag({key: value for (_, key, _, _), value in zip(targets, results)})


def bits_of(count):
    bits = count.bit_length() - 1
    assert 1 << bits == count
    return bits


class Chunk:
    def __init__(self, axis, bits, size, settled=()):
        self.axis = axis
        self.bits = list(range(bits - 1, 0, -1))
        self.size = size
        self.settled = list(settled)
        self.terms = []

    def add(self, term, start=0):
        left = [bit for bit in self.bits if bit not in self.settled]
        self.terms.append((term.reshape((2,) * len(left) + term.shape[-2:]), left, start))

    def take(self, term, start, left, flip):
        me = lax.axis_index(self.axis)
        side = lambda bit: 1 - ((me >> bit) & 1) if bit == flip else (me >> bit) & 1
        starts = [side(bit) if bit in self.settled else 0 for bit in left]
        sizes = [1 if bit in self.settled else 2 for bit in left]
        cols = term.shape[-1]
        piece = lax.dynamic_slice(term, starts + [start, 0], sizes + [self.size, cols])
        open_bits = [2] * (len(self.bits) - len(self.settled))
        return piece.reshape(open_bits + [self.size, cols]).astype(F32)

    def split(self, bit):
        self.settled.append(bit)
        return sum(self.take(term, start, left, bit) for term, left, start in self.terms).astype(
            BF16
        )

    def total(self):
        return sum(self.take(term, start, left, None) for term, left, start in self.terms)


def exchange(block, axis, bit):
    count = lax.axis_size(axis)
    return lax.ppermute(block, axis, [(i, i ^ (1 << bit)) for i in range(count)])


def join(*items):
    return lax.optimization_barrier(items)


def angle_table(span):
    half = HEAD // 2
    freqs = np.exp(-math.log(10000.0) * np.arange(half, dtype=np.float32) / half)
    phase = np.arange(span, dtype=np.float32)[:, None] * freqs.astype(np.float32)[None, :]
    cos_part, sin_part = np.cos(phase), np.sin(phase)
    return np.stack(
        [
            np.concatenate([cos_part] * 4, axis=1),
            np.concatenate([-sin_part, sin_part] * 2, axis=1),
        ]
    ).astype(np.float32)


def per_device(
    ends_in,
    lengths,
    times,
    norm_gain,
    attend_in,
    attend_out,
    time_weight,
    time_bias,
    expand_weight,
    expand_bias,
    reduce_weight,
    reduce_bias,
):
    local = ends_in[0]
    micro = lengths.shape[1]
    assert micro == 2
    width = local.shape[1]
    span = local.shape[0] // micro
    hidden = expand_weight.shape[2]
    count = lax.axis_size("rep")
    section = lax.axis_index("section")
    rank = lax.axis_index("rep")
    core = rank & 1
    steps = jnp.exp(-math.log(10000.0) * jnp.arange(EMB // 2, dtype=F32) / (EMB // 2))
    turn = times.reshape(micro * SEGS, 1).astype(F32) * steps
    embed = jnp.concatenate([jnp.cos(turn), jnp.sin(turn)], axis=1)
    mods = jnp.dot(embed, time_weight[0].astype(F32), precision=lax.Precision.HIGHEST)
    fused = width // count % 16 == 0 and TILE % (hidden // count) == 0 and count >= 16
    common = Bag(
        args=(
            lengths[0],
            section.reshape(1),
            core.reshape(1),
            mods,
            time_bias,
            jnp.asarray(angle_table(span)),
            norm_gain,
            expand_bias,
            reduce_bias,
        ),
        sizes=(span, width, hidden, count),
        tokens=local.shape[0],
        cores=2 if fused else 1,
    )
    weights = Bag(
        win=attend_in[0], wout=attend_out[0], wex=expand_weight[0], wre=reduce_weight[0]
    )
    rows = [(local, slot * span) for slot in range(micro)]
    same = lambda *names: {name: name for name in names}
    whole = same("left", "bg", "pa", "jg")
    run = partial(stage, common=common)
    both = (forward, output, mlp, copy_agrad, attend)
    over = lambda block, route: lax.ppermute(block, "section", route)
    swap = lambda block, bit: exchange(block, "rep", bit)
    a = run(
        "first_0",
        parts=(forward,),
        who=0,
        slot=0,
        loads=dict(xv=rows[0], **weights),
        stores=dict(result="leave"),
        kept=False,
    )
    came_0 = over(a.leave, [(0, 1)])
    b = run(
        "first_1",
        parts=(forward,),
        who=0,
        slot=1,
        loads=dict(xv=rows[1], **weights),
        stores=same("result", "left", "qkv", "probs", "middle", "slope", "branch"),
        after=(a.leave,),
        heads_step=1,
    )
    came_1 = over(b.result, [(0, 1)])
    x = run(
        "second_0",
        parts=both,
        who=1,
        slot=0,
        loads=dict(xv=came_0, dyv=rows[0], **weights),
        stores=dict(whole, result=("ends", 0), leave="leave"),
        after=(b.result,),
        heads_step=6,
    )
    back_0 = over(x.leave, [(1, 0)])
    y = run(
        "second_1",
        parts=both,
        who=1,
        slot=1,
        loads=dict(xv=came_1, dyv=rows[1], **weights),
        stores=dict(whole, result=("ends", span), leave="leave"),
        carried=dict(b, ends=x.ends),
        after=(x.leave,),
        heads_step=6,
    )
    back_1 = over(y.leave, [(1, 0)])
    gates = mods[SEGS : 2 * SEGS, 2 * width :] + time_bias[:, 2 * width :].astype(F32)
    gates = jnp.where(lengths[0, 1, 0] == span, gates[:1], gates)
    after = (y.leave, gates)
    if fused:
        turned, _ = join(embed.T, y.leave)
        embeds = (turned, swap(turned, 0))
        after += (embeds[1],)
    x = run(
        "back_0",
        parts=both,
        who=0,
        slot=0,
        loads=dict(xv=rows[0], dyv=back_0, **weights),
        stores=dict(whole, leave=("ends", 0)),
        carried=dict(x, ends=y.ends),
        after=after,
        heads_step=2,
    )
    if fused:
        y_left = swap(y.left_send, 0)
        back_1, x_send, x_bg = join(back_1, x.left_send, x.bg)
        lefts = [x.left, y.left, swap(x_send, 0), y_left]
        others = [swap(item, 0) for item in (x_bg, x.pa, x.jg)]
    cotan = back_1.astype(F32).reshape(SEGS, -1, width)
    made = (cotan * gates[:, None]).reshape(span, width).astype(BF16)
    bg_1 = jnp.where(section == 0, made, y.bg)
    after = ()
    if fused:
        bg_1_other = swap(bg_1, 0)
        after = (bg_1_other, others[0], lefts[2], lefts[3])
    part = run(
        "back_1_mlp",
        parts=(mlp,),
        who=0,
        slot=1,
        loads=dict(
            bg=bg_1,
            wre=weights.wre,
            slope=b.slope,
            wex=weights.wex,
            middle=b.middle,
            dyv=back_1,
            branch=b.branch,
        ),
        stores=same("pa", "middle_grad"),
        carried=y,
        after=after,
        pieces=dict(wre=(0, hidden // width), slope=(1, hidden // width), wex=(1, hidden // width)),
    )
    pa_1 = part.pa
    bits = bits_of(count)
    term = partial(term_call, sizes=common.sizes, core=core, rank=rank)
    lines = width // count
    deep = EMB // count
    sizes = (hidden // count, hidden // count + lines + 3 * deep + TAIL_ROWS, 3 * lines + GAIN_ROWS)
    bases = left_bases(width, hidden)

    def last_attend(after):
        return run(
            "back_1_attend",
            parts=(attend,),
            who=0,
            slot=1,
            loads=dict(
                agrad=(pa_1, None, (hidden, width)),
                wout=weights.wout,
                probs=b.probs,
                qkv=b.qkv,
                win=weights.win,
                xv=rows[1],
                middle_grad=part.middle_grad,
            ),
            stores=dict(jg="jg", leave=("ends", span)),
            carried=dict(y, ends=x.ends),
            after=after,
            heads_step=6,
        )

    def pair_of(size, first):
        cut = size // 2 if fused else size // 32 * 16
        one = Chunk("rep", bits, cut, (1,) if fused else ())
        two = Chunk("rep", bits, size - cut, (2,) if fused else ())
        if fused:
            send_1, keep_1, send_2, keep_2 = first
            one.add(keep_1)
            two.add(keep_2)
            return one, two, send_1, send_2
        view = first.reshape((count // 2, 2) + first.shape[1:])
        cut = lambda at: lax.dynamic_index_in_dim(view, at, 1, keepdims=False)
        came = swap(cut(1 - core).astype(BF16), 0)
        for item in (cut(core), came):
            one.add(item)
            two.add(item, one.size)
        return one, two, one.split(1), two.split(2)

    if fused:
        pa_other = swap(pa_1, 0)
        sent = term(
            "term_reduce",
            term_reduce,
            lines=sizes[0],
            base=bases[0],
            rows=hidden // 2,
            lefts=lefts,
            rights=[x.bg, bg_1, others[0], bg_1_other],
            after=(pa_1,),
        )
        r1, r2, send_1, send_2 = pair_of(sizes[0], sent)
        came_r1, came_r2 = swap(send_1, 1), swap(send_2, 2)
        sent = term(
            "term_expand",
            term_expand,
            lines=sizes[1],
            base=bases[1],
            rows=width,
            lefts=lefts,
            rights=[x.pa, pa_1, others[1], pa_other],
            embeds=embeds,
            after=(send_1, send_2),
        )
        came_r1, came_r2, *sent = join(came_r1, came_r2, *sent)
        e1, e2, send_1, send_2 = pair_of(sizes[1], sent)
        came_e1, came_e2 = swap(send_1, 1), swap(send_2, 2)
        last = last_attend((send_1, send_2))
        jg_1 = last.jg
        jg_other = swap(jg_1, 0)
        came_r1, came_r2, _ = join(came_r1, came_r2, jg_1)
        r1.add(came_r1)
        r2.add(came_r2)
        send_3, send_4 = r1.split(2), r2.split(1)
        came_r1, came_r2 = swap(send_3, 2), swap(send_4, 1)
        came_e1, came_e2, _, _ = join(came_e1, came_e2, send_3, send_4)
        e1.add(came_e1)
        e2.add(came_e2)
        send_1, send_2 = e1.split(2), e2.split(1)
        came_e1, came_e2 = swap(send_1, 2), swap(send_2, 1)
        sent = term(
            "term_attend",
            term_attend,
            lines=sizes[2],
            base=bases[3],
            rows=width // 2,
            lefts=lefts,
            rights=[x.jg, jg_1, others[2], jg_other],
            after=(send_1, send_2, send_3, send_4),
        )
        came_r1, came_r2, *sent = join(came_r1, came_r2, *sent)
        a1, a2, send_1, send_2 = pair_of(sizes[2], sent)
    else:
        last = last_attend(())
        rights = [(x.bg, bg_1), (x.pa, pa_1), (x.jg, last.jg)]
        totals = plain_pieces((x.left, y.left), rights, embed.T, common.sizes)
        r1, r2, send_1, send_2 = pair_of(sizes[0], totals[0])
        r1.add(swap(send_1, 1))
        r2.add(swap(send_2, 2))
        came_r1, came_r2 = swap(r1.split(2), 2), swap(r2.split(1), 1)
        e1, e2, send_1, send_2 = pair_of(sizes[1], totals[1])
        e1.add(swap(send_1, 1))
        e2.add(swap(send_2, 2))
        came_e1, came_e2 = swap(e1.split(2), 2), swap(e2.split(1), 1)
        a1, a2, send_1, send_2 = pair_of(sizes[2], totals[2])
    ends = last.ends
    came_a1, came_a2 = swap(send_1, 1), swap(send_2, 2)
    r1.add(came_r1)
    r2.add(came_r2)
    block_r = jnp.concatenate([r1.split(3), r2.split(3)], axis=-2)
    came_r = swap(block_r, 3)
    came_e1, came_e2, _ = join(came_e1, came_e2, block_r)
    e1.add(came_e1)
    e2.add(came_e2)
    block_e = jnp.concatenate([e1.split(3), e2.split(3)], axis=-2)
    came_e = swap(block_e, 3)
    came_a1, came_a2, _ = join(came_a1, came_a2, block_e)
    a1.add(came_a1)
    a2.add(came_a2)
    send_1, send_2 = a1.split(2), a2.split(1)
    came_a1, came_a2 = swap(send_1, 2), swap(send_2, 1)
    a1.add(came_a1)
    a2.add(came_a2)
    block_a = jnp.concatenate([a1.split(3), a2.split(3)], axis=-2)
    came_a = swap(block_a, 3)
    came_r, _ = join(came_r, send_1)
    r1.add(came_r[..., : r1.size, :])
    r2.add(came_r[..., r1.size :, :])
    came_e, _ = join(came_e, block_a)
    e1.add(came_e[..., : e1.size, :])
    e2.add(came_e[..., e1.size :, :])
    a1.add(came_a[..., : a1.size, :])
    a2.add(came_a[..., a1.size :, :])
    for bit in range(4, bits):
        for chunk in (r1, r2, e1, e2, a1, a2):
            chunk.add(swap(chunk.split(bit), bit))
    share_r, share_e, share_a = (
        jnp.concatenate([one.total(), two.total()]) for one, two in ((r1, r2), (e1, e2), (a1, a2))
    )
    tall = hidden // width
    side = lambda item, n, size: jnp.concatenate(
        [item[i * size : (i + 1) * size] for i in range(n)], axis=1
    )
    at_o = tall * lines
    at_t = at_o + lines
    small = share_e[at_t + 3 * deep :]
    flat = lambda item, first, n: lax.dynamic_slice_in_dim(
        item[first : first + n].reshape(-1), rank * (n * width // count), n * width // count
    )
    results = (
        flat(share_a, 3 * lines, 1),
        side(share_a, 3, lines),
        share_e[at_o:at_t],
        side(share_e[at_t:], 3, deep),
        flat(small, 1, 3),
        side(share_e, tall, lines),
        flat(small, 4, tall),
        share_r,
        flat(small, 0, 1),
    )
    return (ends[None],) + tuple(piece[None] for piece in results)


def solution(mesh):
    return jax.shard_map(
        per_device,
        mesh=mesh,
        in_specs=(
            P("section", "rep", None),
            P("rep", None, None),
            P("rep", None, None),
            P("section", None),
            P("section", None, None),
            P("section", None, None),
            P("section", None, None),
            P("section", None),
            P("section", None, None),
            P("section", None),
            P("section", None, None),
            P("section", None),
        ),
        out_specs=(
            P("section", "rep", None),
            P("section", "rep"),
            P("section", "rep", None),
            P("section", "rep", None),
            P("section", "rep", None),
            P("section", "rep"),
            P("section", "rep", None),
            P("section", "rep"),
            P("section", "rep", None),
            P("section", "rep"),
        ),
        check_vma=False,
    )
```

profile of v0, /device:TPU:0, one launch (start us, length us, event | category | flops | bytes accessed | tf_op | source)
XLA Modules:
  0.0 223.8 jit_solution(12179381489180667023)
XLA Ops:
  1.7 1.0 fusion.1.refs_3_
  2.7 11.3 %first_0.1.refs_14_ = bf16[256,768]{1,0:T(8,128)(2,1)} custom-call(s32[2,4]{1,0:T(2,128)} %bitcast.178, s32[1]{0:T(128)} %bitcast.1.refs_1_, s32[1]{0:T(128)} %bitcast.2.refs_2_.refs_0_, f32[8,2304]{1,0:T(8,128)} %fusion.1.refs_3_, bf16[1,2304]{1,0:T(2,128)(2,1)} %refs_4_.13, f32[2,256,128]{2,1,0:T(8,128)} %constant.44.clone.refs_5_, ...), custom_call_target="tpu_custom_call" | custom-call | tf_op jit(solution)/shard_map/first_0/pallas_call | solution.py:759
  14.0 1.3 collective-permute-start.1
  15.3 18.0 %first_1.1 = (bf16[256,768]{1,0:T(8,128)(2,1)}, bf16[2688,256]{1,0:T(8,128)(2,1)}, bf16[2688,256]{1,0:T(8,128)(2,1)}, bf16[256,2304]{1,0:T(8,128)(2,1)}, f32[12,...) custom-call(s32[2,4]{1,0:T(2,128)} %bitcast.179, s32[1]{0:T(128)} %bitcast.1.refs_1_, ...), custom_call_target="tpu_custom_call" | custom-call | tf_op jit(solution)/shard_map/first_1/pallas_call | solution.py:759
  33.4 1.3 collective-permute-start
  36.1 11.7 %second_0.1 = (bf16[2688,256]{1,0:T(8,128)(2,1)}, bf16[2688,256]{1,0:T(8,128)(2,1)}, bf16[256,768]{1,0:T(8,128)(2,1)}, bf16[272,3840]{1,0:T(8,128)(2,1)}, bf16[2...) custom-call(s32[2,4]{1,0:T(2,128)} %bitcast.180, s32[1]{0:T(128)} %bitcast.1.refs_1_, ...), custom_call_target="tpu_custom_call" | custom-call | tf_op jit(solution)/shard_map/second_0/pallas_call | solution.py:759
  47.8 1.3 collective-permute-start.3
  49.9 6.7 %second_1.1 = (bf16[2688,256]{1,0:T(8,128)(2,1)}, bf16[2688,256]{1,0:T(8,128)(2,1)}, bf16[256,768]{1,0:T(8,128)(2,1)}, bf16[272,3840]{1,0:T(8,128)(2,1)}, bf16[2...) custom-call(s32[2,4]{1,0:T(2,128)} %bitcast.181, ...), custom_call_target="tpu_custom_call", output_to_operand_aliasing={{0}: (15, {}), {1}: (16, {}), {5}: (17, {})} | custom-call | tf_op jit(solution)/shard_map/second_1/pallas_call | solution.py:759
  56.6 1.3 collective-permute-start.2
  60.5 1.3 broadcast_select_fusion.refs_22_
  61.9 9.4 %collective-permute-done.3.refs_10_ = bf16[256,768]{1,0:T(8,128)(2,1)} collective-permute-done((bf16[256,768]{1,0:T(8,128)(2,1)}, bf16[256,768]{1,0:T(8,128)(2,1)}, u32[]{:S(2)}, u32[]{:S(2)}) %collective-permute-start.3) | collective-permute-done | bytes 393248 | tf_op jit(solution)/shard_map/ppermute | solution.py:886
  71.3 24.1 %back_0.1 = (bf16[2688,256]{1,0:T(8,128)(2,1)}, bf16[2688,256]{1,0:T(8,128)(2,1)}, bf16[256,768]{1,0:T(8,128)(2,1)}, bf16[272,3840]{1,0:T(8,128)(2,1)}, bf16[272...) custom-call(s32[2,4]{1,0:T(2,128)} %bitcast.182, ...), custom_call_target="tpu_custom_call", output_to_operand_aliasing={{0}: (15, {}), {1}: (16, {}), {2}: (17, {}), {3}: (18, {}),... | custom-call | tf_op jit(solution)/shard_map/back_0/pallas_call | solution.py:759
  95.4 1.3 collective-permute-done.2.refs_14_
  97.4 1.1 fusion.12.refs_9_.refs_7_
  99.2 1.2 collective-permute-done.5.refs_17_.refs_9_
  100.3 1.3 collective-permute-done.6.refs_18_.refs_8_
  102.9 9.4 %back_1_mlp.1 = (bf16[272,3840]{1,0:T(8,128)(2,1)}, f32[256,768]{1,0:T(8,128)}) custom-call(s32[2,4]{1,0:T(2,128)} %bitcast.183, s32[1]{0:T(128)} %bitcast.1.refs_1_, s32[1]{0:T(128)} %bitcast.2.refs_2_.refs_0_, f32[8,2304]{1,0:T(8,128)} %fusion.1.refs_3_, bf16[1,2304]{1,0:T(2,128)(2,1)} %refs_4_.13, ...), custom_call_target="tpu_custom_call", output_to_operand_aliasing={{0}: (16, {})} | custom-call | tf_op jit(solution)/shard_map/back_1_mlp/pallas_call | solution.py:759
  112.5 7.2 %term_reduce.1 = (bf16[4,96,768]{2,1,0:T(8,128)(2,1)}, f32[4,96,768]{2,1,0:T(8,128)}, bf16[4,96,768]{2,1,0:T(8,128)(2,1)}, f32[4,96,768]{2,1,0:T(8,128)}) custom-call(s32[1]{0:T(128)} %bitcast.2.refs_2_.refs_0_, s32[1]{0:T(128)} %bitcast.12.refs_1_, bf16[2688,256]{1,0:T(8,128)(2,1)} %get-tuple-element.110.refs_2_.refs_4_, ...), custom_call_target="tpu_custom_call" | custom-call | tf_op jit(solution)/shard_map/term_reduce/pallas_call | solution.py:600
  119.7 1.9 collective-permute-start.10
  121.6 1.5 collective-permute-start.9
  123.2 10.3 %term_expand.1 = (bf16[4,144,768]{2,1,0:T(8,128)(2,1)}, f32[4,144,768]{2,1,0:T(8,128)}, bf16[4,144,768]{2,1,0:T(8,128)(2,1)}, f32[4,144,768]{2,1,0:T(8,128)}) custom-call(s32[1]{0:T(128)} %bitcast.2.refs_2_.refs_0_, s32[1]{0:T(128)} %bitcast.12.refs_1_, f32[128,8]{1,0:T(8,128)} %bitcast.177, f32[128,8]{1,0:T(8,128)} %copy-done.20, ...), custom_call_target="tpu_custom_call" | custom-call | tf_op jit(solution)/shard_map/term_expand/pallas_call | solution.py:600
  133.5 2.2 collective-permute-done.10
  135.7 1.6 collective-permute-done.9
  137.2 1.5 collective-permute-start.17
  139.2 11.7 %back_1_attend.1 = (bf16[272,2304]{1,0:T(8,128)(2,1)}, bf16[512,768]{1,0:T(8,128)(2,1)}) custom-call(s32[2,4]{1,0:T(2,128)} %bitcast.184, s32[1]{0:T(128)} %bitcast.1.refs_1_, s32[1]{0:T(128)} %bitcast.2.refs_2_.refs_0_, f32[8,2304]{1,0:T(8,128)} %fusion.1.refs_3_, bf16[1,2304]{1,0:T(2,128)(2,1)} %refs_4_.13, ...), custom_call_target="tpu_custom_call", output_to_operand_aliasing={{0}: (16, {}), {1}: (17, {})} | custom-call | tf_op jit(solution)/shard_map/back_1_attend/pallas_call | solution.py:759
  151.0 2.0 fusion.14.refs_13_
  153.4 2.0 fusion.13.refs_12_
  155.4 4.7 %collective-permute-done.17 = bf16[4,144,768]{2,1,0:T(8,128)(2,1)} collective-permute-done((bf16[4,144,768]{2,1,0:T(8,128)(2,1)}, bf16[4,144,768]{2,1,0:T(8,128)(2,1)}, u32[]{:S(2)}, u32[]{:S(2)}) %collective-permute-start.17) | collective-permute-done | bytes 884768 | tf_op jit(solution)/shard_map/ppermute | solution.py:813
  160.1 1.1 fusion.4.refs_11_
  161.3 2.0 collective-permute-start.22
  163.3 1.9 fusion.3.refs_10_
  165.2 1.6 collective-permute-start.21
  166.8 5.9 %term_attend.1 = (bf16[4,80,768]{2,1,0:T(8,128)(2,1)}, f32[4,80,768]{2,1,0:T(8,128)}, bf16[4,80,768]{2,1,0:T(8,128)(2,1)}, f32[4,80,768]{2,1,0:T(8,128)}) custom-call(s32[1]{0:T(128)} %bitcast.2.refs_2_.refs_0_, s32[1]{0:T(128)} %bitcast.12.refs_1_, bf16[2688,256]{1,0:T(8,128)(2,1)} %get-tuple-element.110.refs_2_.refs_4_, ...), custom_call_target="tpu_custom_call" | custom-call | tf_op jit(solution)/shard_map/term_attend/pallas_call | solution.py:600
  173.3 1.3 fusion.17
  174.6 2.7 %collective-permute-start.27 = (bf16[192,768]{1,0:T(8,128)(2,1)S(1)}, bf16[192,768]{1,0:T(8,128)(2,1)S(1)}, u32[]{:S(2)}, u32[]{:S(2)}) collective-permute-start(bf16[192,768]{1,0:T(8,128)(2,1)S(1)} %pad_maximum_fusion.2), channel_id=1, source_target_pairs={{0,8},{1,9},{2,10},{3,11},{4,12},{5,13},{6,14},{7,15},{8,0},{9,1},... | collective-permute-start | bytes 884744 | tf_op jit(solution)/shard_map/ppermute | solution.py:813
  177.3 13.2 %collective-permute-done.21 = bf16[2,144,768]{2,1,0:T(8,128)(2,1)} collective-permute-done((bf16[2,144,768]{2,1,0:T(8,128)(2,1)}, bf16[2,144,768]{2,1,0:T(8,128)(2,1)}, u32[]{:S(2)}, u32[]{:S(2)}) %collective-permute-start.21) | collective-permute-done | bytes 442400 | tf_op jit(solution)/shard_map/ppermute | solution.py:813
  190.5 1.1 fusion.11
  191.7 1.3 fusion.10
  193.1 5.1 %collective-permute-done.20 = bf16[4,80,768]{2,1,0:T(8,128)(2,1)S(1)} collective-permute-done((bf16[4,80,768]{2,1,0:T(8,128)(2,1)}, bf16[4,80,768]{2,1,0:T(8,128)(2,1)S(1)}, u32[]{:S(2)}, u32[]{:S(2)}) %collective-permute-start.20) | collective-permute-done | bytes 491552 | tf_op jit(solution)/shard_map/ppermute | solution.py:813
  198.4 1.8 collective-permute-start.23
  200.3 1.4 fusion.16
  201.6 0.9 maximum_bitcast_fusion.1
  202.5 4.4 %collective-permute-done.24 = bf16[2,80,768]{2,1,0:T(8,128)(2,1)S(1)} collective-permute-done((bf16[2,80,768]{2,1,0:T(8,128)(2,1)S(1)}, bf16[2,80,768]{2,1,0:T(8,128)(2,1)S(1)}, u32[]{:S(2)}, u32[]{:S(2)}) %collective-permute-start.24) | collective-permute-done | bytes 245792 | tf_op jit(solution)/shard_map/ppermute | solution.py:813
  207.1 2.6 %collective-permute-done.26 = bf16[288,768]{1,0:T(8,128)(2,1)S(1)} collective-permute-done((bf16[288,768]{1,0:T(8,128)(2,1)S(1)}, bf16[288,768]{1,0:T(8,128)(2,1)S(1)}, u32[]{:S(2)}, u32[]{:S(2)}) %collective-permute-start.26) | collective-permute-done | bytes 442400 | tf_op jit(solution)/shard_map/ppermute | solution.py:813
  209.6 1.6 fusion.8
  212.0 1.4 collective-permute-start.25
  216.8 4.2 %collective-permute-done.25 = bf16[160,768]{1,0:T(8,128)(2,1)S(1)} collective-permute-done((bf16[160,768]{1,0:T(8,128)(2,1)S(1)}, bf16[160,768]{1,0:T(8,128)(2,1)S(1)}, u32[]{:S(2)}, u32[]{:S(2)}) %collective-permute-start.25) | collective-permute-done | bytes 245792 | tf_op jit(solution)/shard_map/ppermute | solution.py:813
  220.9 1.2 fusion.21
  (119 shorter events, 15.6 us)
Async XLA Ops:
  14.0 21.4 %collective-permute-start.1 = (bf16[256,768]{1,0:T(8,128)(2,1)}, bf16[256,768]{1,0:T(8,128)(2,1)S(1)}, u32[]{:S(2)}, u32[]{:S(2)}) collective-permute-start(bf16[256,768]{1,0:T(8,128)(2,1)} %first_0.1.refs_14_), channel_id=1, source_target_pairs={{0,16},{1,17},{2,18},{3,19},{4,20},{5,21},{6,22},{7,23},{8,24},{9,... | collective-permute-start | bytes 1179656 | tf_op jit(solution)/shard_map/ppermute | solution.py:886
  33.4 15.8 %collective-permute-start = (bf16[256,768]{1,0:T(8,128)(2,1)}, bf16[256,768]{1,0:T(8,128)(2,1)S(1)}, u32[]{:S(2)}, u32[]{:S(2)}) collective-permute-start(bf16[256,768]{1,0:T(8,128)(2,1)} %get-tuple-element.80.refs_15_), channel_id=1, source_target_pairs={{0,16},{1,17},{2,18},{3,19},{4,20},{5,21},{6,22},{7,23},{8,24},{9,... | collective-permute-start | bytes 1179656 | tf_op jit(solution)/shard_map/ppermute | solution.py:886
  47.8 23.4 %collective-permute-start.3 = (bf16[256,768]{1,0:T(8,128)(2,1)}, bf16[256,768]{1,0:T(8,128)(2,1)}, u32[]{:S(2)}, u32[]{:S(2)}) collective-permute-start(bf16[256,768]{1,0:T(8,128)(2,1)} %get-tuple-element.84.refs_18_), channel_id=1, source_target_pairs={{16,0},{17,1},{18,2},{19,3},{20,4},{21,5},{22,6},{23,7},{24,8},{25... | collective-permute-start | bytes 1179656 | tf_op jit(solution)/shard_map/ppermute | solution.py:886
  49.9 8.9 %copy-start.25 = (s32[1,2,4]{2,1,0:T(2,128)S(1)}, s32[1,2,4]{2,1,0:T(2,128)}, u32[]{:S(2)}) copy-start(s32[1,2,4]{2,1,0:T(2,128)} %param.14) | copy-start | bytes 100
  56.6 40.0 %collective-permute-start.2 = (bf16[256,768]{1,0:T(8,128)(2,1)}, bf16[256,768]{1,0:T(8,128)(2,1)S(1)}, u32[]{:S(2)}, u32[]{:S(2)}) collective-permute-start(bf16[256,768]{1,0:T(8,128)(2,1)} %get-tuple-element.85.refs_21_), channel_id=1, source_target_pairs={{16,0},{17,1},{18,2},{19,3},{20,4},{21,5},{22,6},{23,7},{24,8},{25... | collective-permute-start | bytes 1179656 | tf_op jit(solution)/shard_map/ppermute | solution.py:886
  58.8 36.6 %copy-start.21 = (f32[8,128]{0,1:T(8,128)}, f32[8,128]{0,1:T(8,128)S(1)}, u32[]{:S(2)}) copy-start(f32[8,128]{0,1:T(8,128)S(1)} %copy.35) | copy-start | bytes 12292
  60.0 1.9 collective-permute-start.4
  61.8 39.9 %collective-permute-start.8 = (bf16[2688,256]{1,0:T(8,128)(2,1)}, bf16[2688,256]{1,0:T(8,128)(2,1)S(1)}, u32[]{:S(2)}, u32[]{:S(2)}) collective-permute-start(bf16[2688,256]{1,0:T(8,128)(2,1)} %get-tuple-element.103), channel_id=1, source_target_pairs={{0,1},{1,0},{2,3},{3,2},{4,5},{5,4},{6,7},{7,6},{8,9},{9,8},{10,11... | collective-permute-start | bytes 4128776 | tf_op jit(solution)/shard_map/ppermute | solution.py:813
  61.9 9.4 %copy-start.20 = (f32[128,8]{1,0:T(8,128)}, f32[128,8]{1,0:T(8,128)S(1)}, u32[]{:S(2)}) copy-start(f32[128,8]{1,0:T(8,128)S(1)} %collective-permute-done.4.refs_23_.refs_3_) | copy-start | bytes 12292
  71.3 26.1 %copy-start.24 = (f32[4,768]{1,0:T(4,128)S(1)}, f32[4,768]{1,0:T(4,128)}, u32[]{:S(2)}) copy-start(f32[4,768]{1,0:T(4,128)} %broadcast_select_fusion.refs_22_) | copy-start | bytes 36868
  96.6 5.0 %collective-permute-start.7 = (bf16[2688,256]{1,0:T(8,128)(2,1)}, bf16[2688,256]{1,0:T(8,128)(2,1)}, u32[]{:S(2)}, u32[]{:S(2)}) collective-permute-start(bf16[2688,256]{1,0:T(8,128)(2,1)} %get-tuple-element.102), channel_id=1, source_target_pairs={{0,1},{1,0},{2,3},{3,2},{4,5},{5,4},{6,7},{7,6},{8,9},{9,8},{10,11... | collective-permute-start | bytes 4128776 | tf_op jit(solution)/shard_map/ppermute | solution.py:813
  98.5 3.9 %copy-start.4 = (bf16[256,768]{1,0:T(8,128)(2,1)}, bf16[256,768]{1,0:T(8,128)(2,1)S(1)}, u32[]{:S(2)}) copy-start(bf16[256,768]{1,0:T(8,128)(2,1)S(1)} %fusion.12.refs_9_.refs_7_) | copy-start | bytes 1179652
  98.5 1.8 collective-permute-start.5
  98.6 3.1 %collective-permute-start.6 = (bf16[256,768]{1,0:T(8,128)(2,1)}, bf16[256,768]{1,0:T(8,128)(2,1)S(1)}, u32[]{:S(2)}, u32[]{:S(2)}) collective-permute-start(bf16[256,768]{1,0:T(8,128)(2,1)} %get-tuple-element.101.refs_6_), channel_id=1, source_target_pairs={{0,1},{1,0},{2,3},{3,2},{4,5},{5,4},{6,7},{7,6},{8,9},{9,8},{10,11... | collective-permute-start | bytes 1179656 | tf_op jit(solution)/shard_map/ppermute | solution.py:813
  99.1 24.1 %collective-permute-start.11 = (bf16[272,3840]{1,0:T(8,128)(2,1)}, bf16[272,3840]{1,0:T(8,128)(2,1)}, u32[]{:S(2)}, u32[]{:S(2)}) collective-permute-start(bf16[272,3840]{1,0:T(8,128)(2,1)} %get-tuple-element.114.refs_8_), channel_id=1, source_target_pairs={{0,1},{1,0},{2,3},{3,2},{4,5},{5,4},{6,7},{7,6},{8,9},{9,8},{10,11... | collective-permute-start | bytes 6266888 | tf_op jit(solution)/shard_map/ppermute | solution.py:813
  100.3 1.3 copy-start.9
  112.3 10.8 %collective-permute-start.12 = (bf16[272,3840]{1,0:T(8,128)(2,1)}, bf16[272,3840]{1,0:T(8,128)(2,1)}, u32[]{:S(2)}, u32[]{:S(2)}) collective-permute-start(bf16[272,3840]{1,0:T(8,128)(2,1)} %get-tuple-element.104.refs_10_.refs_9_), channel_id=1, source_target_pairs={{0,1},{1,0},{2,3},{3,2},{4,5},{5,4},{6,7},{7,6},{8,9},{9,8},{10,11... | collective-permute-start | bytes 6266888 | tf_op jit(solution)/shard_map/ppermute | solution.py:813
  112.5 10.6 %copy-start.3 = (bf16[272,2304]{1,0:T(8,128)(2,1)S(1)}, bf16[272,2304]{1,0:T(8,128)(2,1)}, u32[]{:S(2)}) copy-start(bf16[272,2304]{1,0:T(8,128)(2,1)} %get-tuple-element.129.refs_6_) | copy-start | bytes 3760132
  119.7 15.9 %collective-permute-start.10 = (bf16[4,96,768]{2,1,0:T(8,128)(2,1)}, bf16[4,96,768]{2,1,0:T(8,128)(2,1)S(1)}, u32[]{:S(2)}, u32[]{:S(2)}) collective-permute-start(bf16[4,96,768]{2,1,0:T(8,128)(2,1)} %get-tuple-element.113.refs_13_), channel_id=1, source_target_pairs={{0,4},{1,5},{2,6},{3,7},{4,0},{5,1},{6,2},{7,3},{8,12},{9,13},{10,... | collective-permute-start | bytes 1769480 | tf_op jit(solution)/shard_map/ppermute | solution.py:813
  121.6 15.6 %collective-permute-start.9 = (bf16[4,96,768]{2,1,0:T(8,128)(2,1)}, bf16[4,96,768]{2,1,0:T(8,128)(2,1)}, u32[]{:S(2)}, u32[]{:S(2)}) collective-permute-start(bf16[4,96,768]{2,1,0:T(8,128)(2,1)} %get-tuple-element.112.refs_12_), channel_id=1, source_target_pairs={{0,2},{1,3},{2,0},{3,1},{4,6},{5,7},{6,4},{7,5},{8,10},{9,11},{10,... | collective-permute-start | bytes 1769480 | tf_op jit(solution)/shard_map/ppermute | solution.py:813
  123.1 42.0 %collective-permute-start.15 = (bf16[272,2304]{1,0:T(8,128)(2,1)S(1)}, bf16[272,2304]{1,0:T(8,128)(2,1)}, u32[]{:S(2)}, u32[]{:S(2)}) collective-permute-start(bf16[272,2304]{1,0:T(8,128)(2,1)S(1)} %copy-done.3), channel_id=1, source_target_pairs={{0,1},{1,0},{2,3},{3,2},{4,5},{5,4},{6,7},{7,6},{8,9},{9,8},{10,11... | collective-permute-start | bytes 3760136 | tf_op jit(solution)/shard_map/ppermute | solution.py:813
  135.7 15.3 %copy-start.15 = (bf16[4,96,768]{2,1,0:T(8,128)(2,1)}, bf16[4,96,768]{2,1,0:T(8,128)(2,1)S(1)}, u32[]{:S(2)}) copy-start(bf16[4,96,768]{2,1,0:T(8,128)(2,1)S(1)} %collective-permute-done.10) | copy-start | bytes 1769476
  137.2 22.9 %collective-permute-start.17 = (bf16[4,144,768]{2,1,0:T(8,128)(2,1)}, bf16[4,144,768]{2,1,0:T(8,128)(2,1)}, u32[]{:S(2)}, u32[]{:S(2)}) collective-permute-start(bf16[4,144,768]{2,1,0:T(8,128)(2,1)} %get-tuple-element.119.refs_18_), channel_id=1, source_target_pairs={{0,2},{1,3},{2,0},{3,1},{4,6},{5,7},{6,4},{7,5},{8,10},{9,11},{10,... | collective-permute-start | bytes 2654216 | tf_op jit(solution)/shard_map/ppermute | solution.py:813
  138.8 21.4 %collective-permute-start.18 = (bf16[4,144,768]{2,1,0:T(8,128)(2,1)}, bf16[4,144,768]{2,1,0:T(8,128)(2,1)}, u32[]{:S(2)}, u32[]{:S(2)}) collective-permute-start(bf16[4,144,768]{2,1,0:T(8,128)(2,1)} %get-tuple-element.120.refs_19_), channel_id=1, source_target_pairs={{0,4},{1,5},{2,6},{3,7},{4,0},{5,1},{6,2},{7,3},{8,12},{9,13},{10,... | collective-permute-start | bytes 2654216 | tf_op jit(solution)/shard_map/ppermute | solution.py:813
  150.9 15.9 %collective-permute-start.16 = (bf16[272,2304]{1,0:T(8,128)(2,1)}, bf16[272,2304]{1,0:T(8,128)(2,1)}, u32[]{:S(2)}, u32[]{:S(2)}) collective-permute-start(bf16[272,2304]{1,0:T(8,128)(2,1)} %get-tuple-element.125.refs_7_), channel_id=1, source_target_pairs={{0,1},{1,0},{2,3},{3,2},{4,5},{5,4},{6,7},{7,6},{8,9},{9,8},{10,11... | collective-permute-start | bytes 3760136 | tf_op jit(solution)/shard_map/ppermute | solution.py:813
  151.0 9.2 %copy-start.7 = (f32[4,144,768]{2,1,0:T(8,128)S(1)}, f32[4,144,768]{2,1,0:T(8,128)}, u32[]{:S(2)}) copy-start(f32[4,144,768]{2,1,0:T(8,128)} %get-tuple-element.132) | copy-start | bytes 5308420
  153.0 19.7 %collective-permute-start.14 = (bf16[2,96,768]{2,1,0:T(8,128)(2,1)}, bf16[2,96,768]{2,1,0:T(8,128)(2,1)}, u32[]{:S(2)}, u32[]{:S(2)}) collective-permute-start(bf16[2,96,768]{2,1,0:T(8,128)(2,1)} %fusion.14.refs_13_), channel_id=1, source_target_pairs={{0,2},{1,3},{2,0},{3,1},{4,6},{5,7},{6,4},{7,5},{8,10},{9,11},{10,... | collective-permute-start | bytes 884744 | tf_op jit(solution)/shard_map/ppermute | solution.py:813
  153.4 9.9 %copy-start.5 = (f32[4,144,768]{2,1,0:T(8,128)S(1)}, f32[4,144,768]{2,1,0:T(8,128)}, u32[]{:S(2)}) copy-start(f32[4,144,768]{2,1,0:T(8,128)} %get-tuple-element.130) | copy-start | bytes 5308420
  160.1 12.6 %collective-permute-start.13 = (bf16[2,96,768]{2,1,0:T(8,128)(2,1)}, bf16[2,96,768]{2,1,0:T(8,128)(2,1)}, u32[]{:S(2)}, u32[]{:S(2)}) collective-permute-start(bf16[2,96,768]{2,1,0:T(8,128)(2,1)} %fusion.13.refs_12_), channel_id=1, source_target_pairs={{0,4},{1,5},{2,6},{3,7},{4,0},{5,1},{6,2},{7,3},{8,12},{9,13},{10,... | collective-permute-start | bytes 884744 | tf_op jit(solution)/shard_map/ppermute | solution.py:813
  161.3 5.5 %copy-start.8 = (bf16[2,144,768]{2,1,0:T(8,128)(2,1)}, bf16[2,144,768]{2,1,0:T(8,128)(2,1)S(1)}, u32[]{:S(2)}) copy-start(bf16[2,144,768]{2,1,0:T(8,128)(2,1)S(1)} %fusion.4.refs_11_) | copy-start | bytes 1327108
  161.3 16.0 %collective-permute-start.22 = (bf16[2,144,768]{2,1,0:T(8,128)(2,1)S(1)}, bf16[2,144,768]{2,1,0:T(8,128)(2,1)}, u32[]{:S(2)}, u32[]{:S(2)}) collective-permute-start(bf16[2,144,768]{2,1,0:T(8,128)(2,1)S(1)} %fusion.4.refs_11_), channel_id=1, source_target_pairs={{0,2},{1,3},{2,0},{3,1},{4,6},{5,7},{6,4},{7,5},{8,10},{9,11},{10,... | collective-permute-start | bytes 1327112 | tf_op jit(solution)/shard_map/ppermute | solution.py:813
  165.2 25.4 %collective-permute-start.21 = (bf16[2,144,768]{2,1,0:T(8,128)(2,1)}, bf16[2,144,768]{2,1,0:T(8,128)(2,1)}, u32[]{:S(2)}, u32[]{:S(2)}) collective-permute-start(bf16[2,144,768]{2,1,0:T(8,128)(2,1)} %fusion.3.refs_10_), channel_id=1, source_target_pairs={{0,4},{1,5},{2,6},{3,7},{4,0},{5,1},{6,2},{7,3},{8,12},{9,13},{10,... | collective-permute-start | bytes 1327112 | tf_op jit(solution)/shard_map/ppermute | solution.py:813
  166.7 6.6 %copy-start.12 = (f32[4,96,768]{2,1,0:T(8,128)S(1)}, f32[4,96,768]{2,1,0:T(8,128)}, u32[]{:S(2)}) copy-start(f32[4,96,768]{2,1,0:T(8,128)} %get-tuple-element.122) | copy-start | bytes 3538948
  172.7 17.9 %copy-start.6 = (f32[4,144,768]{2,1,0:T(8,128)S(1)}, f32[4,144,768]{2,1,0:T(8,128)}, u32[]{:S(2)}) copy-start(f32[4,144,768]{2,1,0:T(8,128)} %get-tuple-element.130) | copy-start | bytes 5308420
  172.7 20.4 %collective-permute-start.19 = (bf16[4,80,768]{2,1,0:T(8,128)(2,1)}, bf16[4,80,768]{2,1,0:T(8,128)(2,1)S(1)}, u32[]{:S(2)}, u32[]{:S(2)}) collective-permute-start(bf16[4,80,768]{2,1,0:T(8,128)(2,1)} %get-tuple-element.139), channel_id=1, source_target_pairs={{0,2},{1,3},{2,0},{3,1},{4,6},{5,7},{6,4},{7,5},{8,10},{9,11},{10,... | collective-permute-start | bytes 1474568 | tf_op jit(solution)/shard_map/ppermute | solution.py:813
  173.3 24.9 %collective-permute-start.20 = (bf16[4,80,768]{2,1,0:T(8,128)(2,1)}, bf16[4,80,768]{2,1,0:T(8,128)(2,1)S(1)}, u32[]{:S(2)}, u32[]{:S(2)}) collective-permute-start(bf16[4,80,768]{2,1,0:T(8,128)(2,1)} %get-tuple-element.140), channel_id=1, source_target_pairs={{0,4},{1,5},{2,6},{3,7},{4,0},{5,1},{6,2},{7,3},{8,12},{9,13},{10,... | collective-permute-start | bytes 1474568 | tf_op jit(solution)/shard_map/ppermute | solution.py:813
  174.6 23.6 %copy-start.13 = (f32[4,80,768]{2,1,0:T(8,128)S(1)}, f32[4,80,768]{2,1,0:T(8,128)}, u32[]{:S(2)}) copy-start(f32[4,80,768]{2,1,0:T(8,128)} %get-tuple-element.146) | copy-start | bytes 2949124
  174.6 23.7 %collective-permute-start.27 = (bf16[192,768]{1,0:T(8,128)(2,1)S(1)}, bf16[192,768]{1,0:T(8,128)(2,1)S(1)}, u32[]{:S(2)}, u32[]{:S(2)}) collective-permute-start(bf16[192,768]{1,0:T(8,128)(2,1)S(1)} %pad_maximum_fusion.2), channel_id=1, source_target_pairs={{0,8},{1,9},{2,10},{3,11},{4,12},{5,13},{6,14},{7,15},{8,0},{9,1},... | collective-permute-start | bytes 884744 | tf_op jit(solution)/shard_map/ppermute | solution.py:813
  191.6 6.7 %copy-start.14 = (f32[4,80,768]{2,1,0:T(8,128)S(1)}, f32[4,80,768]{2,1,0:T(8,128)}, u32[]{:S(2)}) copy-start(f32[4,80,768]{2,1,0:T(8,128)} %get-tuple-element.138) | copy-start | bytes 2949124
  193.0 16.6 %collective-permute-start.26 = (bf16[288,768]{1,0:T(8,128)(2,1)S(1)}, bf16[288,768]{1,0:T(8,128)(2,1)S(1)}, u32[]{:S(2)}, u32[]{:S(2)}) collective-permute-start(bf16[288,768]{1,0:T(8,128)(2,1)S(1)} %pad_maximum_fusion.1), channel_id=1, source_target_pairs={{0,8},{1,9},{2,10},{3,11},{4,12},{5,13},{6,14},{7,15},{8,0},{9,1},... | collective-permute-start | bytes 1327112 | tf_op jit(solution)/shard_map/ppermute | solution.py:813
  193.1 13.8 %copy-start.16 = (bf16[4,80,768]{2,1,0:T(8,128)(2,1)}, bf16[4,80,768]{2,1,0:T(8,128)(2,1)S(1)}, u32[]{:S(2)}) copy-start(bf16[4,80,768]{2,1,0:T(8,128)(2,1)S(1)} %collective-permute-done.19) | copy-start | bytes 1474564
  198.2 8.8 %copy-start.17 = (bf16[4,80,768]{2,1,0:T(8,128)(2,1)}, bf16[4,80,768]{2,1,0:T(8,128)(2,1)S(1)}, u32[]{:S(2)}) copy-start(bf16[4,80,768]{2,1,0:T(8,128)(2,1)S(1)} %collective-permute-done.20) | copy-start | bytes 1474564
  198.3 8.6 %collective-permute-start.24 = (bf16[2,80,768]{2,1,0:T(8,128)(2,1)S(1)}, bf16[2,80,768]{2,1,0:T(8,128)(2,1)S(1)}, u32[]{:S(2)}, u32[]{:S(2)}) collective-permute-start(bf16[2,80,768]{2,1,0:T(8,128)(2,1)S(1)} %fusion.20), channel_id=1, source_target_pairs={{0,4},{1,5},{2,6},{3,7},{4,0},{5,1},{6,2},{7,3},{8,12},{9,13},{10,... | collective-permute-start | bytes 737288 | tf_op jit(solution)/shard_map/ppermute | solution.py:813
  198.4 8.5 %collective-permute-start.23 = (bf16[2,80,768]{2,1,0:T(8,128)(2,1)S(1)}, bf16[2,80,768]{2,1,0:T(8,128)(2,1)S(1)}, u32[]{:S(2)}, u32[]{:S(2)}) collective-permute-start(bf16[2,80,768]{2,1,0:T(8,128)(2,1)S(1)} %fusion.19), channel_id=1, source_target_pairs={{0,2},{1,3},{2,0},{3,1},{4,6},{5,7},{6,4},{7,5},{8,10},{9,11},{10,... | collective-permute-start | bytes 737288 | tf_op jit(solution)/shard_map/ppermute | solution.py:813
  207.0 4.3 %copy-start.22 = (bf16[2,80,768]{2,1,0:T(8,128)(2,1)}, bf16[2,80,768]{2,1,0:T(8,128)(2,1)S(1)}, u32[]{:S(2)}) copy-start(bf16[2,80,768]{2,1,0:T(8,128)(2,1)S(1)} %collective-permute-done.23) | copy-start | bytes 737284
  211.9 9.0 %copy-start.23 = (bf16[2,80,768]{2,1,0:T(8,128)(2,1)S(1)}, bf16[2,80,768]{2,1,0:T(8,128)(2,1)}, u32[]{:S(2)}) copy-start(bf16[2,80,768]{2,1,0:T(8,128)(2,1)} %copy-done.22) | copy-start | bytes 737284
  212.0 9.0 %collective-permute-start.25 = (bf16[160,768]{1,0:T(8,128)(2,1)S(1)}, bf16[160,768]{1,0:T(8,128)(2,1)S(1)}, u32[]{:S(2)}, u32[]{:S(2)}) collective-permute-start(bf16[160,768]{1,0:T(8,128)(2,1)S(1)} %pad_maximum_fusion.3), channel_id=1, source_target_pairs={{0,8},{1,9},{2,10},{3,11},{4,12},{5,13},{6,14},{7,15},{8,0},{9,1},... | collective-permute-start | bytes 737288 | tf_op jit(solution)/shard_map/ppermute | solution.py:813
  216.1 7.4 %copy-start.1 = (bf16[1,128,2304]{2,1,0:T(8,128)(2,1)S(1)}, bf16[1,128,2304]{2,1,0:T(8,128)(2,1)}, u32[]{:S(2)}) copy-start(bf16[1,128,2304]{2,1,0:T(8,128)(2,1)} %param.19) | copy-start | bytes 1769476
  (6 other events, 5.3 us)
where the time goes:
time: 228 us; the launch traced here: 224 us
  Pallas kernels  116 us (51%)
  waiting for transfers between devices  51 us (22%)
  other arithmetic  23.1 us (10%)
  starting transfers between devices  22.8 us (10%)
  local copies, waits for them, and re-layouts  7.48 us (3%)
    pallas_call x7, Pallas kernels, stage(): pl.pallas_call(partial(stage_kernel, common.sizes, parts, who, slot, plan...  92.9 us
    ppermute x24, waiting for transfers between devices, exchange(): return lax.ppermute(block, axis, [(i, i ^ 1 << bit) for i in range(count)])  40.4 us
    pallas_call x3, Pallas kernels, term_call(): pl.pallas_call(partial(term_kernel, sizes, body, base, len(after)), out_s...  23.4 us
    ppermute x24, starting transfers between devices, exchange(): return lax.ppermute(block, axis, [(i, i ^ 1 << bit) for i in range(count)])  17.5 us
    convert_element_type x11, other arithmetic, split(): sum((self.take(term, start, left, bit) for term, left, start in self.terms))  10.9 us
    ppermute x4, waiting for transfers between devices, per_device(): over = lambda block, route: lax.ppermute(block, 'section', route)  10.6 us
    ppermute x4, starting transfers between devices, per_device(): over = lambda block, route: lax.ppermute(block, 'section', route)  5.21 us
  transfers between devices with their start and end apart: 28, of which 12 were waited for; matrix products, arithmetic and copies ran while one was open for 9% of the time, Pallas kernels for 47%

commit v1 on v0

--- a/solution.py
+++ b/solution.py
@@ -893,6 +893,7 @@
         loads=dict(xv=rows[0], **weights),
         stores=dict(result="leave"),
         kept=False,
+        heads_step=6,
     )
     came_0 = over(a.leave, [(0, 1)])
     b = run(
@@ -945,7 +946,7 @@
         stores=dict(whole, leave=("ends", 0)),
         carried=dict(x, ends=y.ends),
         after=after,
-        heads_step=2,
+        heads_step=3,
     )
     if fused:
         y_left = swap(y.left_send, 0)

time: 228 us -> 228 us (level)
  no operation moved by 1% of the time
where the time goes in v1:
time: 228 us; the launch traced here: 224 us
  Pallas kernels  115 us (50%)
  waiting for transfers between devices  51.7 us (23%)
  other arithmetic  23.1 us (10%)
  starting transfers between devices  22.7 us (10%)
  local copies, waits for them, and re-layouts  7.48 us (3%)
    pallas_call x7, Pallas kernels, stage(): pl.pallas_call(partial(stage_kernel, common.sizes, parts, who, slot, plan...  92 us
    ppermute x24, waiting for transfers between devices, exchange(): return lax.ppermute(block, axis, [(i, i ^ 1 << bit) for i in range(count)])  40.5 us
    pallas_call x3, Pallas kernels, term_call(): pl.pallas_call(partial(term_kernel, sizes, body, base, len(after)), out_s...  23.4 us
    ppermute x24, starting transfers between devices, exchange(): return lax.ppermute(block, axis, [(i, i ^ 1 << bit) for i in range(count)])  17.5 us
    ppermute x4, waiting for transfers between devices, per_device(): over = lambda block, route: lax.ppermute(block, 'section', route)  11.3 us
    convert_element_type x11, other arithmetic, split(): sum((self.take(term, start, left, bit) for term, left, start in self.terms))  10.9 us
    ppermute x4, starting transfers between devices, per_device(): over = lambda block, route: lax.ppermute(block, 'section', route)  5.21 us
  transfers between devices with their start and end apart: 28, of which 12 were waited for; matrix products, arithmetic and copies ran while one was open for 9% of the time, Pallas kernels for 47%

profile of v1, /device:TPU:0, one launch (start us, length us, event | category | flops | bytes accessed | tf_op | source)
XLA Modules:
  0.0 223.6 jit_solution(9501273140160910692)
XLA Ops:
  1.7 1.0 fusion.1.refs_3_
  2.7 11.1 %first_0.1.refs_14_ = bf16[256,768]{1,0:T(8,128)(2,1)} custom-call(s32[2,4]{1,0:T(2,128)} %bitcast.178, s32[1]{0:T(128)} %bitcast.1.refs_1_, s32[1]{0:T(128)} %bitcast.2.refs_2_.refs_0_, f32[8,2304]{1,0:T(8,128)} %fusion.1.refs_3_, bf16[1,2304]{1,0:T(2,128)(2,1)} %refs_4_.13, f32[2,256,128]{2,1,0:T(8,128)} %constant.44.clone.refs_5_, ...), custom_call_target="tpu_custom_call" | custom-call | tf_op jit(solution)/shard_map/first_0/pallas_call | solution.py:759
  13.8 1.3 collective-permute-start.1
  15.1 18.0 %first_1.1 = (bf16[256,768]{1,0:T(8,128)(2,1)}, bf16[2688,256]{1,0:T(8,128)(2,1)}, bf16[2688,256]{1,0:T(8,128)(2,1)}, bf16[256,2304]{1,0:T(8,128)(2,1)}, f32[12,...) custom-call(s32[2,4]{1,0:T(2,128)} %bitcast.179, s32[1]{0:T(128)} %bitcast.1.refs_1_, ...), custom_call_target="tpu_custom_call" | custom-call | tf_op jit(solution)/shard_map/first_1/pallas_call | solution.py:759
  33.1 1.3 collective-permute-start
  35.9 11.7 %second_0.1 = (bf16[2688,256]{1,0:T(8,128)(2,1)}, bf16[2688,256]{1,0:T(8,128)(2,1)}, bf16[256,768]{1,0:T(8,128)(2,1)}, bf16[272,3840]{1,0:T(8,128)(2,1)}, bf16[2...) custom-call(s32[2,4]{1,0:T(2,128)} %bitcast.180, s32[1]{0:T(128)} %bitcast.1.refs_1_, ...), custom_call_target="tpu_custom_call" | custom-call | tf_op jit(solution)/shard_map/second_0/pallas_call | solution.py:759
  47.6 1.3 collective-permute-start.3
  49.6 7.2 %second_1.1 = (bf16[2688,256]{1,0:T(8,128)(2,1)}, bf16[2688,256]{1,0:T(8,128)(2,1)}, bf16[256,768]{1,0:T(8,128)(2,1)}, bf16[272,3840]{1,0:T(8,128)(2,1)}, bf16[2...) custom-call(s32[2,4]{1,0:T(2,128)} %bitcast.181, ...), custom_call_target="tpu_custom_call", output_to_operand_aliasing={{0}: (15, {}), {1}: (16, {}), {5}: (17, {})} | custom-call | tf_op jit(solution)/shard_map/second_1/pallas_call | solution.py:759
  56.8 1.3 collective-permute-start.2
  60.7 1.3 broadcast_select_fusion.refs_22_
  62.1 8.9 %collective-permute-done.3.refs_10_ = bf16[256,768]{1,0:T(8,128)(2,1)} collective-permute-done((bf16[256,768]{1,0:T(8,128)(2,1)}, bf16[256,768]{1,0:T(8,128)(2,1)}, u32[]{:S(2)}, u32[]{:S(2)}) %collective-permute-start.3) | collective-permute-done | bytes 393248 | tf_op jit(solution)/shard_map/ppermute | solution.py:886
  71.0 23.0 %back_0.1 = (bf16[2688,256]{1,0:T(8,128)(2,1)}, bf16[2688,256]{1,0:T(8,128)(2,1)}, bf16[256,768]{1,0:T(8,128)(2,1)}, bf16[272,3840]{1,0:T(8,128)(2,1)}, bf16[272...) custom-call(s32[2,4]{1,0:T(2,128)} %bitcast.182, ...), custom_call_target="tpu_custom_call", output_to_operand_aliasing={{0}: (15, {}), {1}: (16, {}), {2}: (17, {}), {3}: (18, {}),... | custom-call | tf_op jit(solution)/shard_map/back_0/pallas_call | solution.py:759
  94.1 2.3 %collective-permute-done.2.refs_14_ = bf16[256,768]{1,0:T(8,128)(2,1)S(1)} collective-permute-done((bf16[256,768]{1,0:T(8,128)(2,1)}, bf16[256,768]{1,0:T(8,128)(2,1)S(1)}, u32[]{:S(2)}, u32[]{:S(2)}) %collective-permute-start.2) | collective-permute-done | bytes 393248 | tf_op jit(solution)/shard_map/ppermute | solution.py:886
  97.2 1.1 fusion.12.refs_9_.refs_7_
  98.9 1.2 collective-permute-done.5.refs_17_.refs_9_
  100.1 1.3 collective-permute-done.6.refs_18_.refs_8_
  102.6 9.4 %back_1_mlp.1 = (bf16[272,3840]{1,0:T(8,128)(2,1)}, f32[256,768]{1,0:T(8,128)}) custom-call(s32[2,4]{1,0:T(2,128)} %bitcast.183, s32[1]{0:T(128)} %bitcast.1.refs_1_, s32[1]{0:T(128)} %bitcast.2.refs_2_.refs_0_, f32[8,2304]{1,0:T(8,128)} %fusion.1.refs_3_, bf16[1,2304]{1,0:T(2,128)(2,1)} %refs_4_.13, ...), custom_call_target="tpu_custom_call", output_to_operand_aliasing={{0}: (16, {})} | custom-call | tf_op jit(solution)/shard_map/back_1_mlp/pallas_call | solution.py:759
  112.3 7.2 %term_reduce.1 = (bf16[4,96,768]{2,1,0:T(8,128)(2,1)}, f32[4,96,768]{2,1,0:T(8,128)}, bf16[4,96,768]{2,1,0:T(8,128)(2,1)}, f32[4,96,768]{2,1,0:T(8,128)}) custom-call(s32[1]{0:T(128)} %bitcast.2.refs_2_.refs_0_, s32[1]{0:T(128)} %bitcast.12.refs_1_, bf16[2688,256]{1,0:T(8,128)(2,1)} %get-tuple-element.110.refs_2_.refs_4_, ...), custom_call_target="tpu_custom_call" | custom-call | tf_op jit(solution)/shard_map/term_reduce/pallas_call | solution.py:600
  119.5 1.9 collective-permute-start.10
  121.4 1.5 collective-permute-start.9
  122.9 10.3 %term_expand.1 = (bf16[4,144,768]{2,1,0:T(8,128)(2,1)}, f32[4,144,768]{2,1,0:T(8,128)}, bf16[4,144,768]{2,1,0:T(8,128)(2,1)}, f32[4,144,768]{2,1,0:T(8,128)}) custom-call(s32[1]{0:T(128)} %bitcast.2.refs_2_.refs_0_, s32[1]{0:T(128)} %bitcast.12.refs_1_, f32[128,8]{1,0:T(8,128)} %bitcast.177, f32[128,8]{1,0:T(8,128)} %copy-done.20, ...), custom_call_target="tpu_custom_call" | custom-call | tf_op jit(solution)/shard_map/term_expand/pallas_call | solution.py:600
  133.3 2.2 collective-permute-done.10
  135.4 1.6 collective-permute-done.9
  137.0 1.5 collective-permute-start.17
  139.0 11.7 %back_1_attend.1 = (bf16[272,2304]{1,0:T(8,128)(2,1)}, bf16[512,768]{1,0:T(8,128)(2,1)}) custom-call(s32[2,4]{1,0:T(2,128)} %bitcast.184, s32[1]{0:T(128)} %bitcast.1.refs_1_, s32[1]{0:T(128)} %bitcast.2.refs_2_.refs_0_, f32[8,2304]{1,0:T(8,128)} %fusion.1.refs_3_, bf16[1,2304]{1,0:T(2,128)(2,1)} %refs_4_.13, ...), custom_call_target="tpu_custom_call", output_to_operand_aliasing={{0}: (16, {}), {1}: (17, {})} | custom-call | tf_op jit(solution)/shard_map/back_1_attend/pallas_call | solution.py:759
  150.8 2.0 fusion.14.refs_13_
  153.2 2.0 fusion.13.refs_12_
  155.2 4.7 %collective-permute-done.17 = bf16[4,144,768]{2,1,0:T(8,128)(2,1)} collective-permute-done((bf16[4,144,768]{2,1,0:T(8,128)(2,1)}, bf16[4,144,768]{2,1,0:T(8,128)(2,1)}, u32[]{:S(2)}, u32[]{:S(2)}) %collective-permute-start.17) | collective-permute-done | bytes 884768 | tf_op jit(solution)/shard_map/ppermute | solution.py:813
  159.9 1.1 fusion.4.refs_11_
  161.0 2.0 collective-permute-start.22
  163.1 1.9 fusion.3.refs_10_
  164.9 1.6 collective-permute-start.21
  166.5 5.9 %term_attend.1 = (bf16[4,80,768]{2,1,0:T(8,128)(2,1)}, f32[4,80,768]{2,1,0:T(8,128)}, bf16[4,80,768]{2,1,0:T(8,128)(2,1)}, f32[4,80,768]{2,1,0:T(8,128)}) custom-call(s32[1]{0:T(128)} %bitcast.2.refs_2_.refs_0_, s32[1]{0:T(128)} %bitcast.12.refs_1_, bf16[2688,256]{1,0:T(8,128)(2,1)} %get-tuple-element.110.refs_2_.refs_4_, ...), custom_call_target="tpu_custom_call" | custom-call | tf_op jit(solution)/shard_map/term_attend/pallas_call | solution.py:600
  173.1 1.3 fusion.17
  174.4 2.7 %collective-permute-start.27 = (bf16[192,768]{1,0:T(8,128)(2,1)S(1)}, bf16[192,768]{1,0:T(8,128)(2,1)S(1)}, u32[]{:S(2)}, u32[]{:S(2)}) collective-permute-start(bf16[192,768]{1,0:T(8,128)(2,1)S(1)} %pad_maximum_fusion.2), channel_id=1, source_target_pairs={{0,8},{1,9},{2,10},{3,11},{4,12},{5,13},{6,14},{7,15},{8,0},{9,1},... | collective-permute-start | bytes 884744 | tf_op jit(solution)/shard_map/ppermute | solution.py:813
  177.1 13.3 %collective-permute-done.21 = bf16[2,144,768]{2,1,0:T(8,128)(2,1)} collective-permute-done((bf16[2,144,768]{2,1,0:T(8,128)(2,1)}, bf16[2,144,768]{2,1,0:T(8,128)(2,1)}, u32[]{:S(2)}, u32[]{:S(2)}) %collective-permute-start.21) | collective-permute-done | bytes 442400 | tf_op jit(solution)/shard_map/ppermute | solution.py:813
  190.3 1.1 fusion.11
  191.4 1.3 fusion.10
  192.9 5.1 %collective-permute-done.20 = bf16[4,80,768]{2,1,0:T(8,128)(2,1)S(1)} collective-permute-done((bf16[4,80,768]{2,1,0:T(8,128)(2,1)}, bf16[4,80,768]{2,1,0:T(8,128)(2,1)S(1)}, u32[]{:S(2)}, u32[]{:S(2)}) %collective-permute-start.20) | collective-permute-done | bytes 491552 | tf_op jit(solution)/shard_map/ppermute | solution.py:813
  198.2 1.8 collective-permute-start.23
  200.0 1.4 fusion.16
  201.4 0.9 maximum_bitcast_fusion.1
  202.3 4.4 %collective-permute-done.24 = bf16[2,80,768]{2,1,0:T(8,128)(2,1)S(1)} collective-permute-done((bf16[2,80,768]{2,1,0:T(8,128)(2,1)S(1)}, bf16[2,80,768]{2,1,0:T(8,128)(2,1)S(1)}, u32[]{:S(2)}, u32[]{:S(2)}) %collective-permute-start.24) | collective-permute-done | bytes 245792 | tf_op jit(solution)/shard_map/ppermute | solution.py:813
  206.8 2.6 %collective-permute-done.26 = bf16[288,768]{1,0:T(8,128)(2,1)S(1)} collective-permute-done((bf16[288,768]{1,0:T(8,128)(2,1)S(1)}, bf16[288,768]{1,0:T(8,128)(2,1)S(1)}, u32[]{:S(2)}, u32[]{:S(2)}) %collective-permute-start.26) | collective-permute-done | bytes 442400 | tf_op jit(solution)/shard_map/ppermute | solution.py:813
  209.4 1.6 fusion.8
  211.8 1.4 collective-permute-start.25
  216.6 4.2 %collective-permute-done.25 = bf16[160,768]{1,0:T(8,128)(2,1)S(1)} collective-permute-done((bf16[160,768]{1,0:T(8,128)(2,1)S(1)}, bf16[160,768]{1,0:T(8,128)(2,1)S(1)}, u32[]{:S(2)}, u32[]{:S(2)}) %collective-permute-start.25) | collective-permute-done | bytes 245792 | tf_op jit(solution)/shard_map/ppermute | solution.py:813
  220.8 1.2 fusion.21
  (119 shorter events, 15.6 us)
Async XLA Ops:
  13.8 21.4 %collective-permute-start.1 = (bf16[256,768]{1,0:T(8,128)(2,1)}, bf16[256,768]{1,0:T(8,128)(2,1)S(1)}, u32[]{:S(2)}, u32[]{:S(2)}) collective-permute-start(bf16[256,768]{1,0:T(8,128)(2,1)} %first_0.1.refs_14_), channel_id=1, source_target_pairs={{0,16},{1,17},{2,18},{3,19},{4,20},{5,21},{6,22},{7,23},{8,24},{9,... | collective-permute-start | bytes 1179656 | tf_op jit(solution)/shard_map/ppermute | solution.py:886
  33.1 15.8 %collective-permute-start = (bf16[256,768]{1,0:T(8,128)(2,1)}, bf16[256,768]{1,0:T(8,128)(2,1)S(1)}, u32[]{:S(2)}, u32[]{:S(2)}) collective-permute-start(bf16[256,768]{1,0:T(8,128)(2,1)} %get-tuple-element.80.refs_15_), channel_id=1, source_target_pairs={{0,16},{1,17},{2,18},{3,19},{4,20},{5,21},{6,22},{7,23},{8,24},{9,... | collective-permute-start | bytes 1179656 | tf_op jit(solution)/shard_map/ppermute | solution.py:886
  47.6 23.4 %collective-permute-start.3 = (bf16[256,768]{1,0:T(8,128)(2,1)}, bf16[256,768]{1,0:T(8,128)(2,1)}, u32[]{:S(2)}, u32[]{:S(2)}) collective-permute-start(bf16[256,768]{1,0:T(8,128)(2,1)} %get-tuple-element.84.refs_18_), channel_id=1, source_target_pairs={{16,0},{17,1},{18,2},{19,3},{20,4},{21,5},{22,6},{23,7},{24,8},{25... | collective-permute-start | bytes 1179656 | tf_op jit(solution)/shard_map/ppermute | solution.py:886
  49.6 9.3 %copy-start.25 = (s32[1,2,4]{2,1,0:T(2,128)S(1)}, s32[1,2,4]{2,1,0:T(2,128)}, u32[]{:S(2)}) copy-start(s32[1,2,4]{2,1,0:T(2,128)} %param.14) | copy-start | bytes 100
  56.8 39.6 %collective-permute-start.2 = (bf16[256,768]{1,0:T(8,128)(2,1)}, bf16[256,768]{1,0:T(8,128)(2,1)S(1)}, u32[]{:S(2)}, u32[]{:S(2)}) collective-permute-start(bf16[256,768]{1,0:T(8,128)(2,1)} %get-tuple-element.85.refs_21_), channel_id=1, source_target_pairs={{16,0},{17,1},{18,2},{19,3},{20,4},{21,5},{22,6},{23,7},{24,8},{25... | collective-permute-start | bytes 1179656 | tf_op jit(solution)/shard_map/ppermute | solution.py:886
  59.0 35.1 %copy-start.21 = (f32[8,128]{0,1:T(8,128)}, f32[8,128]{0,1:T(8,128)S(1)}, u32[]{:S(2)}) copy-start(f32[8,128]{0,1:T(8,128)S(1)} %copy.35) | copy-start | bytes 12292
  60.2 1.9 collective-permute-start.4
  62.0 39.4 %collective-permute-start.8 = (bf16[2688,256]{1,0:T(8,128)(2,1)}, bf16[2688,256]{1,0:T(8,128)(2,1)S(1)}, u32[]{:S(2)}, u32[]{:S(2)}) collective-permute-start(bf16[2688,256]{1,0:T(8,128)(2,1)} %get-tuple-element.103), channel_id=1, source_target_pairs={{0,1},{1,0},{2,3},{3,2},{4,5},{5,4},{6,7},{7,6},{8,9},{9,8},{10,11... | collective-permute-start | bytes 4128776 | tf_op jit(solution)/shard_map/ppermute | solution.py:813
  62.1 8.9 %copy-start.20 = (f32[128,8]{1,0:T(8,128)}, f32[128,8]{1,0:T(8,128)S(1)}, u32[]{:S(2)}) copy-start(f32[128,8]{1,0:T(8,128)S(1)} %collective-permute-done.4.refs_23_.refs_3_) | copy-start | bytes 12292
  71.0 26.1 %copy-start.24 = (f32[4,768]{1,0:T(4,128)S(1)}, f32[4,768]{1,0:T(4,128)}, u32[]{:S(2)}) copy-start(f32[4,768]{1,0:T(4,128)} %broadcast_select_fusion.refs_22_) | copy-start | bytes 36868
  96.4 5.0 %collective-permute-start.7 = (bf16[2688,256]{1,0:T(8,128)(2,1)}, bf16[2688,256]{1,0:T(8,128)(2,1)}, u32[]{:S(2)}, u32[]{:S(2)}) collective-permute-start(bf16[2688,256]{1,0:T(8,128)(2,1)} %get-tuple-element.102), channel_id=1, source_target_pairs={{0,1},{1,0},{2,3},{3,2},{4,5},{5,4},{6,7},{7,6},{8,9},{9,8},{10,11... | collective-permute-start | bytes 4128776 | tf_op jit(solution)/shard_map/ppermute | solution.py:813
  98.3 3.9 %copy-start.4 = (bf16[256,768]{1,0:T(8,128)(2,1)}, bf16[256,768]{1,0:T(8,128)(2,1)S(1)}, u32[]{:S(2)}) copy-start(bf16[256,768]{1,0:T(8,128)(2,1)S(1)} %fusion.12.refs_9_.refs_7_) | copy-start | bytes 1179652
  98.3 1.8 collective-permute-start.5
  98.4 3.1 %collective-permute-start.6 = (bf16[256,768]{1,0:T(8,128)(2,1)}, bf16[256,768]{1,0:T(8,128)(2,1)S(1)}, u32[]{:S(2)}, u32[]{:S(2)}) collective-permute-start(bf16[256,768]{1,0:T(8,128)(2,1)} %get-tuple-element.101.refs_6_), channel_id=1, source_target_pairs={{0,1},{1,0},{2,3},{3,2},{4,5},{5,4},{6,7},{7,6},{8,9},{9,8},{10,11... | collective-permute-start | bytes 1179656 | tf_op jit(solution)/shard_map/ppermute | solution.py:813
  98.9 24.0 %collective-permute-start.11 = (bf16[272,3840]{1,0:T(8,128)(2,1)}, bf16[272,3840]{1,0:T(8,128)(2,1)}, u32[]{:S(2)}, u32[]{:S(2)}) collective-permute-start(bf16[272,3840]{1,0:T(8,128)(2,1)} %get-tuple-element.114.refs_8_), channel_id=1, source_target_pairs={{0,1},{1,0},{2,3},{3,2},{4,5},{5,4},{6,7},{7,6},{8,9},{9,8},{10,11... | collective-permute-start | bytes 6266888 | tf_op jit(solution)/shard_map/ppermute | solution.py:813
  100.1 1.3 copy-start.9
  112.1 10.8 %collective-permute-start.12 = (bf16[272,3840]{1,0:T(8,128)(2,1)}, bf16[272,3840]{1,0:T(8,128)(2,1)}, u32[]{:S(2)}, u32[]{:S(2)}) collective-permute-start(bf16[272,3840]{1,0:T(8,128)(2,1)} %get-tuple-element.104.refs_10_.refs_9_), channel_id=1, source_target_pairs={{0,1},{1,0},{2,3},{3,2},{4,5},{5,4},{6,7},{7,6},{8,9},{9,8},{10,11... | collective-permute-start | bytes 6266888 | tf_op jit(solution)/shard_map/ppermute | solution.py:813
  112.3 10.6 %copy-start.3 = (bf16[272,2304]{1,0:T(8,128)(2,1)S(1)}, bf16[272,2304]{1,0:T(8,128)(2,1)}, u32[]{:S(2)}) copy-start(bf16[272,2304]{1,0:T(8,128)(2,1)} %get-tuple-element.129.refs_6_) | copy-start | bytes 3760132
  119.5 16.0 %collective-permute-start.10 = (bf16[4,96,768]{2,1,0:T(8,128)(2,1)}, bf16[4,96,768]{2,1,0:T(8,128)(2,1)S(1)}, u32[]{:S(2)}, u32[]{:S(2)}) collective-permute-start(bf16[4,96,768]{2,1,0:T(8,128)(2,1)} %get-tuple-element.113.refs_13_), channel_id=1, source_target_pairs={{0,4},{1,5},{2,6},{3,7},{4,0},{5,1},{6,2},{7,3},{8,12},{9,13},{10,... | collective-permute-start | bytes 1769480 | tf_op jit(solution)/shard_map/ppermute | solution.py:813
  121.4 15.6 %collective-permute-start.9 = (bf16[4,96,768]{2,1,0:T(8,128)(2,1)}, bf16[4,96,768]{2,1,0:T(8,128)(2,1)}, u32[]{:S(2)}, u32[]{:S(2)}) collective-permute-start(bf16[4,96,768]{2,1,0:T(8,128)(2,1)} %get-tuple-element.112.refs_12_), channel_id=1, source_target_pairs={{0,2},{1,3},{2,0},{3,1},{4,6},{5,7},{6,4},{7,5},{8,10},{9,11},{10,... | collective-permute-start | bytes 1769480 | tf_op jit(solution)/shard_map/ppermute | solution.py:813
  122.9 42.0 %collective-permute-start.15 = (bf16[272,2304]{1,0:T(8,128)(2,1)S(1)}, bf16[272,2304]{1,0:T(8,128)(2,1)}, u32[]{:S(2)}, u32[]{:S(2)}) collective-permute-start(bf16[272,2304]{1,0:T(8,128)(2,1)S(1)} %copy-done.3), channel_id=1, source_target_pairs={{0,1},{1,0},{2,3},{3,2},{4,5},{5,4},{6,7},{7,6},{8,9},{9,8},{10,11... | collective-permute-start | bytes 3760136 | tf_op jit(solution)/shard_map/ppermute | solution.py:813
  135.4 15.3 %copy-start.15 = (bf16[4,96,768]{2,1,0:T(8,128)(2,1)}, bf16[4,96,768]{2,1,0:T(8,128)(2,1)S(1)}, u32[]{:S(2)}) copy-start(bf16[4,96,768]{2,1,0:T(8,128)(2,1)S(1)} %collective-permute-done.10) | copy-start | bytes 1769476
  137.0 22.9 %collective-permute-start.17 = (bf16[4,144,768]{2,1,0:T(8,128)(2,1)}, bf16[4,144,768]{2,1,0:T(8,128)(2,1)}, u32[]{:S(2)}, u32[]{:S(2)}) collective-permute-start(bf16[4,144,768]{2,1,0:T(8,128)(2,1)} %get-tuple-element.119.refs_18_), channel_id=1, source_target_pairs={{0,2},{1,3},{2,0},{3,1},{4,6},{5,7},{6,4},{7,5},{8,10},{9,11},{10,... | collective-permute-start | bytes 2654216 | tf_op jit(solution)/shard_map/ppermute | solution.py:813
  138.5 21.4 %collective-permute-start.18 = (bf16[4,144,768]{2,1,0:T(8,128)(2,1)}, bf16[4,144,768]{2,1,0:T(8,128)(2,1)}, u32[]{:S(2)}, u32[]{:S(2)}) collective-permute-start(bf16[4,144,768]{2,1,0:T(8,128)(2,1)} %get-tuple-element.120.refs_19_), channel_id=1, source_target_pairs={{0,4},{1,5},{2,6},{3,7},{4,0},{5,1},{6,2},{7,3},{8,12},{9,13},{10,... | collective-permute-start | bytes 2654216 | tf_op jit(solution)/shard_map/ppermute | solution.py:813
  150.7 15.8 %collective-permute-start.16 = (bf16[272,2304]{1,0:T(8,128)(2,1)}, bf16[272,2304]{1,0:T(8,128)(2,1)}, u32[]{:S(2)}, u32[]{:S(2)}) collective-permute-start(bf16[272,2304]{1,0:T(8,128)(2,1)} %get-tuple-element.125.refs_7_), channel_id=1, source_target_pairs={{0,1},{1,0},{2,3},{3,2},{4,5},{5,4},{6,7},{7,6},{8,9},{9,8},{10,11... | collective-permute-start | bytes 3760136 | tf_op jit(solution)/shard_map/ppermute | solution.py:813
  150.7 9.2 %copy-start.7 = (f32[4,144,768]{2,1,0:T(8,128)S(1)}, f32[4,144,768]{2,1,0:T(8,128)}, u32[]{:S(2)}) copy-start(f32[4,144,768]{2,1,0:T(8,128)} %get-tuple-element.132) | copy-start | bytes 5308420
  152.7 19.7 %collective-permute-start.14 = (bf16[2,96,768]{2,1,0:T(8,128)(2,1)}, bf16[2,96,768]{2,1,0:T(8,128)(2,1)}, u32[]{:S(2)}, u32[]{:S(2)}) collective-permute-start(bf16[2,96,768]{2,1,0:T(8,128)(2,1)} %fusion.14.refs_13_), channel_id=1, source_target_pairs={{0,2},{1,3},{2,0},{3,1},{4,6},{5,7},{6,4},{7,5},{8,10},{9,11},{10,... | collective-permute-start | bytes 884744 | tf_op jit(solution)/shard_map/ppermute | solution.py:813
  153.2 9.9 %copy-start.5 = (f32[4,144,768]{2,1,0:T(8,128)S(1)}, f32[4,144,768]{2,1,0:T(8,128)}, u32[]{:S(2)}) copy-start(f32[4,144,768]{2,1,0:T(8,128)} %get-tuple-element.130) | copy-start | bytes 5308420
  159.9 12.5 %collective-permute-start.13 = (bf16[2,96,768]{2,1,0:T(8,128)(2,1)}, bf16[2,96,768]{2,1,0:T(8,128)(2,1)}, u32[]{:S(2)}, u32[]{:S(2)}) collective-permute-start(bf16[2,96,768]{2,1,0:T(8,128)(2,1)} %fusion.13.refs_12_), channel_id=1, source_target_pairs={{0,4},{1,5},{2,6},{3,7},{4,0},{5,1},{6,2},{7,3},{8,12},{9,13},{10,... | collective-permute-start | bytes 884744 | tf_op jit(solution)/shard_map/ppermute | solution.py:813
  161.0 5.5 %copy-start.8 = (bf16[2,144,768]{2,1,0:T(8,128)(2,1)}, bf16[2,144,768]{2,1,0:T(8,128)(2,1)S(1)}, u32[]{:S(2)}) copy-start(bf16[2,144,768]{2,1,0:T(8,128)(2,1)S(1)} %fusion.4.refs_11_) | copy-start | bytes 1327108
  161.0 16.0 %collective-permute-start.22 = (bf16[2,144,768]{2,1,0:T(8,128)(2,1)S(1)}, bf16[2,144,768]{2,1,0:T(8,128)(2,1)}, u32[]{:S(2)}, u32[]{:S(2)}) collective-permute-start(bf16[2,144,768]{2,1,0:T(8,128)(2,1)S(1)} %fusion.4.refs_11_), channel_id=1, source_target_pairs={{0,2},{1,3},{2,0},{3,1},{4,6},{5,7},{6,4},{7,5},{8,10},{9,11},{10,... | collective-permute-start | bytes 1327112 | tf_op jit(solution)/shard_map/ppermute | solution.py:813
  164.9 25.4 %collective-permute-start.21 = (bf16[2,144,768]{2,1,0:T(8,128)(2,1)}, bf16[2,144,768]{2,1,0:T(8,128)(2,1)}, u32[]{:S(2)}, u32[]{:S(2)}) collective-permute-start(bf16[2,144,768]{2,1,0:T(8,128)(2,1)} %fusion.3.refs_10_), channel_id=1, source_target_pairs={{0,4},{1,5},{2,6},{3,7},{4,0},{5,1},{6,2},{7,3},{8,12},{9,13},{10,... | collective-permute-start | bytes 1327112 | tf_op jit(solution)/shard_map/ppermute | solution.py:813
  166.5 6.6 %copy-start.12 = (f32[4,96,768]{2,1,0:T(8,128)S(1)}, f32[4,96,768]{2,1,0:T(8,128)}, u32[]{:S(2)}) copy-start(f32[4,96,768]{2,1,0:T(8,128)} %get-tuple-element.122) | copy-start | bytes 3538948
  172.4 17.9 %copy-start.6 = (f32[4,144,768]{2,1,0:T(8,128)S(1)}, f32[4,144,768]{2,1,0:T(8,128)}, u32[]{:S(2)}) copy-start(f32[4,144,768]{2,1,0:T(8,128)} %get-tuple-element.130) | copy-start | bytes 5308420
  172.5 20.4 %collective-permute-start.19 = (bf16[4,80,768]{2,1,0:T(8,128)(2,1)}, bf16[4,80,768]{2,1,0:T(8,128)(2,1)S(1)}, u32[]{:S(2)}, u32[]{:S(2)}) collective-permute-start(bf16[4,80,768]{2,1,0:T(8,128)(2,1)} %get-tuple-element.139), channel_id=1, source_target_pairs={{0,2},{1,3},{2,0},{3,1},{4,6},{5,7},{6,4},{7,5},{8,10},{9,11},{10,... | collective-permute-start | bytes 1474568 | tf_op jit(solution)/shard_map/ppermute | solution.py:813
  173.0 24.9 %collective-permute-start.20 = (bf16[4,80,768]{2,1,0:T(8,128)(2,1)}, bf16[4,80,768]{2,1,0:T(8,128)(2,1)S(1)}, u32[]{:S(2)}, u32[]{:S(2)}) collective-permute-start(bf16[4,80,768]{2,1,0:T(8,128)(2,1)} %get-tuple-element.140), channel_id=1, source_target_pairs={{0,4},{1,5},{2,6},{3,7},{4,0},{5,1},{6,2},{7,3},{8,12},{9,13},{10,... | collective-permute-start | bytes 1474568 | tf_op jit(solution)/shard_map/ppermute | solution.py:813
  174.4 23.6 %copy-start.13 = (f32[4,80,768]{2,1,0:T(8,128)S(1)}, f32[4,80,768]{2,1,0:T(8,128)}, u32[]{:S(2)}) copy-start(f32[4,80,768]{2,1,0:T(8,128)} %get-tuple-element.146) | copy-start | bytes 2949124
  174.4 23.7 %collective-permute-start.27 = (bf16[192,768]{1,0:T(8,128)(2,1)S(1)}, bf16[192,768]{1,0:T(8,128)(2,1)S(1)}, u32[]{:S(2)}, u32[]{:S(2)}) collective-permute-start(bf16[192,768]{1,0:T(8,128)(2,1)S(1)} %pad_maximum_fusion.2), channel_id=1, source_target_pairs={{0,8},{1,9},{2,10},{3,11},{4,12},{5,13},{6,14},{7,15},{8,0},{9,1},... | collective-permute-start | bytes 884744 | tf_op jit(solution)/shard_map/ppermute | solution.py:813
  191.4 6.7 %copy-start.14 = (f32[4,80,768]{2,1,0:T(8,128)S(1)}, f32[4,80,768]{2,1,0:T(8,128)}, u32[]{:S(2)}) copy-start(f32[4,80,768]{2,1,0:T(8,128)} %get-tuple-element.138) | copy-start | bytes 2949124
  192.8 16.6 %collective-permute-start.26 = (bf16[288,768]{1,0:T(8,128)(2,1)S(1)}, bf16[288,768]{1,0:T(8,128)(2,1)S(1)}, u32[]{:S(2)}, u32[]{:S(2)}) collective-permute-start(bf16[288,768]{1,0:T(8,128)(2,1)S(1)} %pad_maximum_fusion.1), channel_id=1, source_target_pairs={{0,8},{1,9},{2,10},{3,11},{4,12},{5,13},{6,14},{7,15},{8,0},{9,1},... | collective-permute-start | bytes 1327112 | tf_op jit(solution)/shard_map/ppermute | solution.py:813
  192.9 13.7 %copy-start.16 = (bf16[4,80,768]{2,1,0:T(8,128)(2,1)}, bf16[4,80,768]{2,1,0:T(8,128)(2,1)S(1)}, u32[]{:S(2)}) copy-start(bf16[4,80,768]{2,1,0:T(8,128)(2,1)S(1)} %collective-permute-done.19) | copy-start | bytes 1474564
  198.0 8.7 %copy-start.17 = (bf16[4,80,768]{2,1,0:T(8,128)(2,1)}, bf16[4,80,768]{2,1,0:T(8,128)(2,1)S(1)}, u32[]{:S(2)}) copy-start(bf16[4,80,768]{2,1,0:T(8,128)(2,1)S(1)} %collective-permute-done.20) | copy-start | bytes 1474564
  198.0 8.6 %collective-permute-start.24 = (bf16[2,80,768]{2,1,0:T(8,128)(2,1)S(1)}, bf16[2,80,768]{2,1,0:T(8,128)(2,1)S(1)}, u32[]{:S(2)}, u32[]{:S(2)}) collective-permute-start(bf16[2,80,768]{2,1,0:T(8,128)(2,1)S(1)} %fusion.20), channel_id=1, source_target_pairs={{0,4},{1,5},{2,6},{3,7},{4,0},{5,1},{6,2},{7,3},{8,12},{9,13},{10,... | collective-permute-start | bytes 737288 | tf_op jit(solution)/shard_map/ppermute | solution.py:813
  198.2 8.5 %collective-permute-start.23 = (bf16[2,80,768]{2,1,0:T(8,128)(2,1)S(1)}, bf16[2,80,768]{2,1,0:T(8,128)(2,1)S(1)}, u32[]{:S(2)}, u32[]{:S(2)}) collective-permute-start(bf16[2,80,768]{2,1,0:T(8,128)(2,1)S(1)} %fusion.19), channel_id=1, source_target_pairs={{0,2},{1,3},{2,0},{3,1},{4,6},{5,7},{6,4},{7,5},{8,10},{9,11},{10,... | collective-permute-start | bytes 737288 | tf_op jit(solution)/shard_map/ppermute | solution.py:813
  206.7 4.3 %copy-start.22 = (bf16[2,80,768]{2,1,0:T(8,128)(2,1)}, bf16[2,80,768]{2,1,0:T(8,128)(2,1)S(1)}, u32[]{:S(2)}) copy-start(bf16[2,80,768]{2,1,0:T(8,128)(2,1)S(1)} %collective-permute-done.23) | copy-start | bytes 737284
  211.7 9.1 %copy-start.23 = (bf16[2,80,768]{2,1,0:T(8,128)(2,1)S(1)}, bf16[2,80,768]{2,1,0:T(8,128)(2,1)}, u32[]{:S(2)}) copy-start(bf16[2,80,768]{2,1,0:T(8,128)(2,1)} %copy-done.22) | copy-start | bytes 737284
  211.8 9.0 %collective-permute-start.25 = (bf16[160,768]{1,0:T(8,128)(2,1)S(1)}, bf16[160,768]{1,0:T(8,128)(2,1)S(1)}, u32[]{:S(2)}, u32[]{:S(2)}) collective-permute-start(bf16[160,768]{1,0:T(8,128)(2,1)S(1)} %pad_maximum_fusion.3), channel_id=1, source_target_pairs={{0,8},{1,9},{2,10},{3,11},{4,12},{5,13},{6,14},{7,15},{8,0},{9,1},... | collective-permute-start | bytes 737288 | tf_op jit(solution)/shard_map/ppermute | solution.py:813
  215.9 7.4 %copy-start.1 = (bf16[1,128,2304]{2,1,0:T(8,128)(2,1)S(1)}, bf16[1,128,2304]{2,1,0:T(8,128)(2,1)}, u32[]{:S(2)}) copy-start(bf16[1,128,2304]{2,1,0:T(8,128)(2,1)} %param.19) | copy-start | bytes 1769476
  (6 other events, 5.3 us)
